TPU v7x, 256 devices: a whole 4x4x8 slice. The times are simulated.
256 devices in a mesh: space: 64 (over z, x, core), tm: 4 (over y).
Axes of the slice: x: 4, y: 4, z: 8, core: 2. Of those that a mesh axis runs over, the one named last changes fastest.
Arguments:
- archive: float32 [512, 524288], P('tm', 'space'), may hold values from -64 to 64
- leaf_sketch: float32 [128, 64], replicated, may hold values from -0.5 to 0.5
- merge_sketch: float32 [128, 64], replicated, may hold values from -0.5 to 0.5
Outputs:
- modes: float32 [64, 524288], P('tm', 'space')
All inputs are finite; a program needn't handle non-finite values.
Results may differ from a plain program's by a relative error of at most 0.0003.
Values sent between devices are 32-bit elements; how exact they have to be, the bound alone decides.
No kernel may reach another device: no remote copies, remote signals or barrier semaphores. Data moves between devices by JAX's collectives and lax.ppermute only.
A program may use at most 192 MiB of HBM per device.

v0:
```python
import jax
import jax.numpy as jnp
from jax import lax
from jax.sharding import PartitionSpec as P


def partner(value, axis, distance):
    mask = 2**distance
    pairs = [(source, source ^ mask) for source in range(lax.axis_size(axis))]
    return lax.ppermute(value, axis, pairs)


def contract(former, latter):
    return lax.dot_general(
        former, latter, (((1,), (1,)), ((), ())), precision=lax.Precision.HIGHEST
    )


def merge_piece(stacked, sketch, reduce_fn):
    highest = lax.Precision.HIGHEST
    sketched = jnp.dot(sketch.T, stacked, precision=highest)
    lower_y = jnp.linalg.cholesky(reduce_fn(contract(sketched, sketched)))
    basis = jax.scipy.linalg.solve_triangular(lower_y, sketched, lower=True)
    mixed_rows = reduce_fn(contract(basis, stacked))
    lower_k = jnp.linalg.cholesky(contract(mixed_rows, mixed_rows))
    return jnp.dot(lower_k.T, basis, precision=highest)


def sum_cells(matrix):
    return lax.psum(matrix, "space")


def on_device(archive, leaf_sketch, merge_sketch):
    tm_count = lax.axis_size("tm")
    tm_index = lax.axis_index("tm")
    levels = tm_count.bit_length() - 1
    snap_rows = archive.shape[0]
    cell_count = archive.shape[1]
    rank = leaf_sketch.shape[1]
    own_rows = rank // tm_count
    per_source = snap_rows // tm_count
    parted = archive.reshape(tm_count, per_source, cell_count)
    arrived = lax.all_to_all(parted, "tm", split_axis=0, concat_axis=0, tiled=True).reshape(
        snap_rows, cell_count
    )
    ordered_sketch = (
        leaf_sketch.reshape(per_source, tm_count, rank).transpose(1, 0, 2).reshape(snap_rows, rank)
    )
    piece = merge_piece(arrived, ordered_sketch, sum_cells)
    for tier_index in range(levels):
        other = partner(piece, "tm", tier_index)
        on_top = tm_index >> tier_index & 1 == 0
        lower_part = jnp.where(on_top, piece, other)
        upper_part = jnp.where(on_top, other, piece)
        stacked = jnp.concatenate([lower_part, upper_part], 0)
        piece = merge_piece(stacked, merge_sketch, sum_cells)
    return lax.dynamic_slice_in_dim(piece, tm_index * own_rows, own_rows, 0)


def solution(mesh):
    in_specs = (P("tm", "space"), P(), P())
    out_specs = P("tm", "space")
    return jax.shard_map(
        on_device, mesh=mesh, in_specs=in_specs, out_specs=out_specs, check_vma=False
    )
```

profile of v0, /device:TPU:1, one launch (start us, length us, event | category | flops | bytes accessed | tf_op | source)
XLA Modules:
  0.0 1739.0 jit_solution(6455670971333475265)
XLA Ops:
  0.0 5.1 all-to-all-start
  5.2 47.0 %all-to-all-done = f32[4,32,8192]{2,1,0:T(8,128)} async-done(((f32[4,32,8192]{2,1,0:T(8,128)}), f32[4,32,8192]{2,1,0:T(8,128)}, u32[]{:S(2)}, u32[]{:S(2)}) %all-to-all-start) | async-done | bytes 4194336 | tf_op jit(solution)/shard_map/all_to_all | solution.py:43
  52.2 4.1 convolution_bitcast_fusion
  58.1 250.5 %psum.42 = f32[64,64]{0,1:T(8,128)S(1)} all-reduce(f32[64,64]{0,1:T(8,128)S(1)} %fusion.62), channel_id=1, replica_groups=mesh['space'=64,'tm'=4] {'space'}, use_global_device_ids=true, to_apply=%region_0.0 | all-reduce | flops 4096 | bytes 32768 | tf_op jit(solution)/shard_map/psum | solution.py:30
  308.7 5.8 cholesky.104
  315.8 4.9 custom-call.7
  320.7 1.9 fusion.19
  324.0 6.2 fusion.63
  330.2 246.7 %psum.43 = f32[64,128]{1,0:T(8,128)S(1)} all-reduce(f32[64,128]{1,0:T(8,128)S(1)} %fusion.63), channel_id=1, replica_groups=mesh['space'=64,'tm'=4] {'space'}, use_global_device_ids=true, to_apply=%region_3.6 | all-reduce | flops 8192 | bytes 65536 | tf_op jit(solution)/shard_map/psum | solution.py:30
  577.2 5.8 cholesky.115
  583.7 4.1 fusion.37
  588.3 41.1 %collective-permute-done = f32[64,8192]{1,0:T(8,128)} collective-permute-done((f32[64,8192]{1,0:T(8,128)S(1)}, f32[64,8192]{1,0:T(8,128)}, u32[]{:S(2)}, u32[]{:S(2)}) %collective-permute-start) | collective-permute-done | bytes 2097184 | tf_op jit(solution)/shard_map/ppermute | solution.py:10
  629.5 2.0 broadcast_select_fusion.1
  631.5 2.5 fusion.3
  635.8 249.2 %psum.44 = f32[64,64]{0,1:T(8,128)S(1)} all-reduce(f32[64,64]{0,1:T(8,128)S(1)} %fusion.65), channel_id=1, replica_groups=mesh['space'=64,'tm'=4] {'space'}, use_global_device_ids=true, to_apply=%region_4.7 | all-reduce | flops 4096 | bytes 32768 | tf_op jit(solution)/shard_map/psum | solution.py:30
  885.1 5.8 cholesky.126
  892.2 4.9 custom-call.8
  900.4 4.4 fusion.2
  904.9 246.1 %psum.45 = f32[64,128]{1,0:T(8,128)S(1)} all-reduce(f32[64,128]{1,0:T(8,128)S(1)} %fusion.2), channel_id=1, replica_groups=mesh['space'=64,'tm'=4] {'space'}, use_global_device_ids=true, to_apply=%region_5.8 | all-reduce | flops 8192 | bytes 65536 | tf_op jit(solution)/shard_map/psum | solution.py:30
  1151.3 5.8 cholesky.137
  1157.8 4.1 fusion.39
  1162.7 42.7 %collective-permute-done.1 = f32[64,8192]{1,0:T(8,128)} collective-permute-done((f32[64,8192]{1,0:T(8,128)S(1)}, f32[64,8192]{1,0:T(8,128)}, u32[]{:S(2)}, u32[]{:S(2)}) %collective-permute-start.1) | collective-permute-done | bytes 2097184 | tf_op jit(solution)/shard_map/ppermute | solution.py:10
  1205.3 2.0 broadcast_select_fusion.3
  1207.3 2.5 fusion.1
  1211.6 249.0 %psum.46 = f32[64,64]{0,1:T(8,128)S(1)} all-reduce(f32[64,64]{0,1:T(8,128)S(1)} %fusion.67), channel_id=1, replica_groups=mesh['space'=64,'tm'=4] {'space'}, use_global_device_ids=true, to_apply=%region_6.9 | all-reduce | flops 4096 | bytes 32768 | tf_op jit(solution)/shard_map/psum | solution.py:30
  1460.7 5.8 cholesky.148
  1467.9 4.9 custom-call.9
  1472.8 1.9 fusion.4
  1476.1 4.4 fusion
  1480.6 246.4 %psum.47 = f32[64,128]{1,0:T(8,128)S(1)} all-reduce(f32[64,128]{1,0:T(8,128)S(1)} %fusion), channel_id=1, replica_groups=mesh['space'=64,'tm'=4] {'space'}, use_global_device_ids=true, to_apply=%region_7.10 | all-reduce | flops 8192 | bytes 65536 | tf_op jit(solution)/shard_map/psum | solution.py:30
  1727.3 5.8 cholesky.159
  1733.8 4.1 fusion.22
  (64 shorter events, 20.5 us)
Async XLA Ops:
  0.0 631.5 %copy-start = (f32[128,64]{0,1:T(8,128)S(1)}, f32[128,64]{0,1:T(8,128)}, u32[]{:S(2)}) copy-start(f32[128,64]{0,1:T(8,128)} %param.8) | copy-start | bytes 98308
  0.0 5.1 copy-start.12
  0.0 52.2 %all-to-all-start = ((f32[4,32,8192]{2,1,0:T(8,128)}), f32[4,32,8192]{2,1,0:T(8,128)}, u32[]{:S(2)}, u32[]{:S(2)}) async-start(f32[4,32,8192]{2,1,0:T(8,128)} %bitcast.75), calls=%async_computation | async-start | bytes 8388608 | tf_op jit(solution)/shard_map/all_to_all | solution.py:43
  322.7 1.3 copy-start.11
  587.8 41.7 %collective-permute-start = (f32[64,8192]{1,0:T(8,128)S(1)}, f32[64,8192]{1,0:T(8,128)}, u32[]{:S(2)}, u32[]{:S(2)}) collective-permute-start(f32[64,8192]{1,0:T(8,128)S(1)} %fusion.37), channel_id=1, source_target_pairs={{0,1},{1,0},{2,3},{3,2},{4,5},{5,4},{6,7},{7,6},{8,9},{9,8},{10,11... | collective-permute-start | bytes 6291464 | tf_op jit(solution)/shard_map/ppermute | solution.py:10
  631.4 2.5 copy-start.1
  631.5 2.5 copy-start.3
  897.1 3.3 copy-start.2
  897.2 3.3 copy-start.4
  899.1 1.4 copy-start.9
  1162.0 43.4 %collective-permute-start.1 = (f32[64,8192]{1,0:T(8,128)S(1)}, f32[64,8192]{1,0:T(8,128)}, u32[]{:S(2)}, u32[]{:S(2)}) collective-permute-start(f32[64,8192]{1,0:T(8,128)S(1)} %fusion.39), channel_id=1, source_target_pairs={{0,2},{1,3},{2,0},{3,1},{4,6},{5,7},{6,4},{7,5},{8,10},{9,11},{10,... | collective-permute-start | bytes 6291464 | tf_op jit(solution)/shard_map/ppermute | solution.py:10
  1207.3 2.5 copy-start.5
  1207.3 2.5 copy-start.7
  1472.8 3.3 copy-start.6
  1472.8 3.3 copy-start.8
  1474.8 1.4 copy-start.10
where the time goes:
time: 1750 us; the launch traced here: 1740 us
  blocking collectives  1490 us (85%)
  waiting for transfers between devices  131 us (7%)
  other arithmetic  59.7 us (3%)
  matrix products  48.2 us (3%)
    psum x6, blocking collectives, sum_cells(): return lax.psum(matrix, 'space')  1490 us
    ppermute x2, waiting for transfers between devices, partner(): return lax.ppermute(value, axis, pairs)  83.8 us
    all_to_all x1, waiting for transfers between devices, on_device(): lax.all_to_all(parted, 'tm', split_axis=0, concat_axis=0, tiled=True)  47 us
  transfers between devices with their start and end apart: 3, of which 3 were waited for; matrix products, arithmetic and copies ran while one was open for 0% of the time, Pallas kernels for 0%

commit v1 on v0

v1 whole, which is shorter than its diff:
```python
import functools

import jax
import jax.numpy as jnp
from jax import lax
from jax.experimental import pallas as pl
from jax.experimental.pallas import tpu as pltpu
from jax.sharding import Mesh, PartitionSpec as P

HI = lax.Precision.HIGHEST
SUB = 8
VMEM = pl.BlockSpec(memory_space=pltpu.VMEM)
SMEM = pl.BlockSpec(memory_space=pltpu.SMEM)
SPACE = ("z", "x", "core")
PARAMS = pltpu.CompilerParams(vmem_limit_bytes=40 * 2**20)


def mm(a, b):
    return jnp.dot(a, b, precision=HI, preferred_element_type=jnp.float32)


def mmt(a, b):
    return lax.dot_general(a, b, (((1,), (1,)), ((), ())), precision=HI, preferred_element_type=jnp.float32)


def mtm(a, b):
    return lax.dot_general(a, b, (((0,), (0,)), ((), ())), precision=HI, preferred_element_type=jnp.float32)


def eliminate(mats, width):
    n, lanes = mats[0].shape
    count = n // SUB
    rows = lax.broadcasted_iota(jnp.int32, (SUB, lanes), 0)
    work = [[m[b * SUB : (b + 1) * SUB, :] for b in range(count)] for m in mats]

    def row(v, c):
        return jnp.broadcast_to(v[c : c + 1, :], (SUB, lanes))

    for first in range(0, n, width):
        p, off = divmod(first, SUB)
        spread = [
            [
                {b: jnp.broadcast_to(w[b][:, first + c : first + c + 1], (SUB, lanes)) for b in range(p, count)}
                for c in range(width)
            ]
            for w in work
        ]
        for c in range(width):
            at = off + c
            for w, t in zip(work, spread):
                inverse = 1.0 / row(t[c][p], at)
                pivot_row = row(w[p], at) * inverse
                for later in range(c + 1, width):
                    scale = row(t[c][p], off + later) * inverse
                    for b in range(p, count):
                        t[later][b] = t[later][b] - t[c][b] * scale
                below = jnp.where(rows > at, t[c][p], 0.0)
                w[p] = w[p] - below * pivot_row
                for b in range(p + 1, count):
                    w[b] = w[b] - t[c][b] * pivot_row
                t[c]["d"] = row(t[c][p], at)
        for w, t in zip(work, spread):
            scale = None
            for c in range(width):
                d = t[c]["d"]
                scale = d if scale is None else jnp.where(rows >= off + c, d, scale)
            scaled = w[p] * lax.rsqrt(scale)
            w[p] = jnp.where((rows >= off) & (rows < off + width), scaled, w[p]) if width < SUB else scaled
    return [jnp.concatenate(w, 0) for w in work]


def upper(u):
    r = lax.broadcasted_iota(jnp.int32, u.shape, 0)
    c = lax.broadcasted_iota(jnp.int32, u.shape, 1)
    return jnp.where(c >= r, u, 0.0)


def level(bs, sketch, widths):
    rank = sketch.shape[1]
    eye = (
        lax.broadcasted_iota(jnp.int32, (rank, rank), 0) == lax.broadcasted_iota(jnp.int32, (rank, rank), 1)
    ).astype(jnp.float32)
    aug = [jnp.concatenate([mm(b, sketch), eye], 1) for b in bs]
    inv = [e[:, rank:] for e in eliminate(aug, widths[0])]
    mixed = [mm(i, b) for i, b in zip(inv, bs)]
    grams = [mmt(m, m) for m in mixed]
    fac = [upper(e) for e in eliminate(grams, widths[1])]
    return fac, [mm(f, i) for f, i in zip(fac, inv)]


def pair(fa, fb, cross):
    return jnp.concatenate(
        [jnp.concatenate([mmt(fa, fa), cross], 1), jnp.concatenate([cross.T, mmt(fb, fb)], 1)], 0
    )


def factor_kernel(widths, red_ref, leaf_ref, leaf_t_ref, merge_ref, merge_t_ref, out_ref):
    wl, wm, wmt = leaf_ref[...], merge_ref[...], merge_t_ref[...]
    r = wl.shape[1]
    leaves = [red_ref[w * r : (w + 1) * r, :] for w in range(4)]
    f, p = level(leaves, wl, widths[0])
    x01, x23 = red_ref[4 * r : 5 * r, :r], red_ref[4 * r : 5 * r, r:]
    cross = red_ref[5 * r : 7 * r, :]
    g = [
        pair(f[0], f[1], mmt(mm(p[0], x01), p[1])),
        pair(f[2], f[3], mmt(mm(p[2], x23), p[3])),
    ]
    f1, q1 = level([mm(wmt, x) for x in g], wm, widths[1])
    h = []
    for i in range(2):
        t = mm(q1[i], wmt)
        h.append(jnp.concatenate([mm(t[:, :r], p[2 * i]), mm(t[:, r:], p[2 * i + 1])], 1))
    top = pair(f1[0], f1[1], mmt(mm(h[0], cross), h[1]))
    _, q2 = level([mm(wmt, top)], wm, widths[2])
    t = mm(q2[0], wmt)
    last = [mm(t[:, :r], h[0]), mm(t[:, r:], h[1])]
    for w in range(4):
        out_ref[:, w * 2 * r : (w + 1) * 2 * r] = mm(last[w // 2][:, w % 2 * r : (w % 2 + 1) * r], leaf_t_ref[...])


def factors(red, leaf, merge, widths=((4, 4), (8, 8), (8, 8))):
    r = leaf.shape[1]
    return pl.pallas_call(
        functools.partial(factor_kernel, widths),
        out_shape=jax.ShapeDtypeStruct((r, 4 * leaf.shape[0]), jnp.float32),
        in_specs=[VMEM] * 5,
        out_specs=VMEM,
        compiler_params=PARAMS,
        name="factors",
    )(red, leaf, leaf.T, merge, merge.T)


def dot_rows(a, b):
    return lax.dot_general(a, b, (((1,), (1,)), ((), ())), preferred_element_type=jnp.float32)


def split(x):
    high = x.astype(jnp.bfloat16)
    return high, (x - high.astype(jnp.float32)).astype(jnp.bfloat16)


def gram_kernel(order_ref, leaf_ref, leaf_t_ref, p0, p1, p2, p3, red_ref, high_ref, low_ref):
    for d, part in enumerate((p0, p1, p2, p3)):
        per = part.shape[0] // 4
        for w in range(4):
            at = pl.ds(pl.multiple_of(w * 4 * per + order_ref[d] * per, per), per)
            high, low = split(part[w * per : (w + 1) * per, :])
            high_ref[at, :] = high
            low_ref[at, :] = low
    wl, wlt = leaf_ref[...], leaf_t_ref[...]
    k, r = wl.shape
    ha, hb = high_ref[: 2 * k, :], high_ref[2 * k :, :]
    la, lb = low_ref[: 2 * k, :], low_ref[2 * k :, :]

    def own(h, l):
        mixed = dot_rows(h, l)
        return dot_rows(h, h) + (dot_rows(l, l) + (mixed + mixed.T))

    gaa, gbb = own(ha, la), own(hb, lb)
    gab = dot_rows(ha, hb) + (dot_rows(ha, lb) + dot_rows(la, hb) + dot_rows(la, lb))
    for w, g in enumerate((gaa[:k, :k], gaa[k:, k:], gbb[:k, :k], gbb[k:, k:])):
        red_ref[w * r : (w + 1) * r, :] = mm(wlt, g)
    for at, lane, g in (
        (4, 0, gaa[:k, k:]),
        (4, 1, gbb[:k, k:]),
        (5, 0, gab[:k, :k]),
        (5, 1, gab[:k, k:]),
        (6, 0, gab[k:, :k]),
        (6, 1, gab[k:, k:]),
    ):
        red_ref[at * r : (at + 1) * r, lane * r : (lane + 1) * r] = mm(mm(wlt, g), wl)
    red_ref[7 * r :, :] = jnp.zeros((r, k), jnp.float32)


def grams(order, leaf, parts):
    k, r = leaf.shape
    cells = parts[0].shape[1]
    return pl.pallas_call(
        gram_kernel,
        out_shape=(
            jax.ShapeDtypeStruct((8 * r, k), jnp.float32),
            jax.ShapeDtypeStruct((4 * k, cells), jnp.bfloat16),
            jax.ShapeDtypeStruct((4 * k, cells), jnp.bfloat16),
        ),
        in_specs=[SMEM] + [VMEM] * 6,
        out_specs=(VMEM,) * 3,
        compiler_params=PARAMS,
        name="grams",
    )(order, leaf, leaf.T, *parts)


def modes_kernel(coef_ref, high_ref, low_ref, out_ref):
    ch, cl = split(coef_ref[...])

    def dot(a, b):
        return jnp.dot(a, b, preferred_element_type=jnp.float32)

    out_ref[...] = dot(ch, high_ref[...]) + (dot(ch, low_ref[...]) + dot(cl, high_ref[...]))


def modes(coef, high, low):
    return pl.pallas_call(
        modes_kernel,
        out_shape=jax.ShapeDtypeStruct((coef.shape[0], high.shape[1]), jnp.float32),
        in_specs=[VMEM] * 3,
        out_specs=VMEM,
        compiler_params=PARAMS,
        name="modes",
    )(coef, high, low)


def place_kernel(order_ref, p0, p1, p2, p3, out_ref):
    cells = p0.shape[1]
    for d, part in enumerate((p0, p1, p2, p3)):
        out_ref[:, pl.ds(pl.multiple_of(order_ref[d] * cells, cells), cells)] = part[...]


def place(order, parts):
    rows, cells = parts[0].shape
    return pl.pallas_call(
        place_kernel,
        out_shape=jax.ShapeDtypeStruct((rows, 4 * cells), jnp.float32),
        in_specs=[SMEM] + [VMEM] * 4,
        out_specs=VMEM,
        compiler_params=PARAMS,
        name="place",
    )(order, *parts)


def ring(axis, step):
    n = lax.axis_size(axis)
    return [(i, (i + step) % n) for i in range(n)]


def a2a(v, axis):
    return lax.all_to_all(v, axis, 0, 0, tiled=True)


def spread_over(v, axis):
    n = lax.axis_size(axis)
    return a2a(jnp.broadcast_to(v[None], (n, *v.shape)), axis)


def sum_everywhere(v):
    rows, lanes = v.shape
    core = lax.axis_index("core")
    half = v.reshape(2, rows // 2, lanes)
    mine = lax.dynamic_index_in_dim(half, core, 0, keepdims=False)
    theirs = lax.dynamic_index_in_dim(half, 1 - core, 0, keepdims=False)
    v = mine + lax.ppermute(theirs, "core", ring("core", 1))
    n = lax.axis_size("z")
    v = a2a(v.reshape(n, rows // 2 // n, lanes), "z").sum(0)
    v = spread_over(v, ("x", "tm")).sum(0)
    v = spread_over(v, "z").reshape(rows // 2, lanes)
    other = lax.ppermute(v, "core", ring("core", 1))
    return jnp.concatenate([jnp.where(core == 0, v, other), jnp.where(core == 0, other, v)], 0)


def on_device(archive, leaf_sketch, merge_sketch):
    t = lax.axis_index("tm")
    n = lax.axis_size("tm")
    k, r = leaf_sketch.shape
    cells = archive.shape[1] // n
    leaf = leaf_sketch.reshape(k // n, n, r).transpose(1, 0, 2).reshape(k, r)
    order = (t - jnp.arange(n, dtype=jnp.int32)) % n

    def chunk(d):
        return lax.dynamic_slice_in_dim(archive, (t + d) % n * cells, cells, 1)

    parts = [chunk(0)] + [None] * (n - 1)
    for d in (1, n - 1, *range(2, n - 1)):
        parts[d] = lax.ppermute(chunk(d), "tm", ring("tm", d))
    red, high, low = grams(order, leaf, parts)
    coef = factors(sum_everywhere(red), leaf, merge_sketch)
    rows = r // n
    out = modes(coef, high, low).reshape(n, rows, cells)

    def share(d):
        return lax.dynamic_index_in_dim(out, (t + d) % n, 0, keepdims=False)

    back = [share(0)] + [None] * (n - 1)
    for d in (1, n - 1, *range(2, n - 1)):
        back[d] = lax.ppermute(share(d), "tm", ring("tm", d))
    return place(order, back)


def solution(mesh):
    fine = Mesh(mesh.devices.reshape(mesh.devices.shape[0] // 8, 4, 2, 4), (*SPACE, "tm"))
    return jax.shard_map(
        on_device, mesh=fine, in_specs=(P("tm", SPACE), P(), P()), out_specs=P("tm", SPACE), check_vma=False
    )
```

time: 1750 us -> 146 us (0.08)
  blocking collectives: 1490 us -> 38.8 us
  waiting for transfers between devices: 131 us -> 50.5 us
  other arithmetic: 59.7 us -> 0.11 us
  matrix products: 48.2 us -> 0 us
  Pallas kernels: 0 us -> 29 us
    psum x6 -> x0, blocking collectives: 1490 us -> none  [sum_cells(): return lax.psum(matrix, 'space')]
    another operation x24 -> x0, other arithmetic: 55.8 us -> none  [the longest x9 19.6 us: merge_piece(): lower_y = jnp.linalg.cholesky(reduce_fn(contract(sketched, sketched)))]
    all_to_all x1 -> x0, waiting for transfers between devices: 47 us -> none  [on_device(): lax.all_to_all(parted, 'tm', split_axis=0, concat_axis=0, tiled=True)]
    dot_general x15 -> x0, matrix products: 42.4 us -> none  [the longest x9 21 us: contract(): lax.dot_general(former, latter, (((1,), (1,)), ((), ())), precision=lax.P...]
    all_to_all x0 -> x3, blocking collectives: none -> 38.8 us  [a2a(): return lax.all_to_all(v, axis, 0, 0, tiled=True)]
    ppermute x2 -> x8, waiting for transfers between devices: 83.8 us -> 50.5 us  [the longest x3 43 us: on_device(): parts[d] = lax.ppermute(chunk(d), 'tm', ring('tm', d))]
    pallas_call x0 -> x4, Pallas kernels: none -> 29 us  [the longest x1 20 us: factors(): pl.pallas_call(functools.partial(factor_kernel, widths), out_shape=jax.Sh...]
  transfers between devices with their start and end apart: 3 -> 8, of which waited for: 3 -> 7; matrix products, arithmetic and copies ran while one was open for 0% -> 0% of each run, Pallas kernels for 0% -> 0%
where the time goes in v1:
time: 146 us
  waiting for transfers between devices  50.5 us (35%)
  blocking collectives  38.8 us (27%)
  Pallas kernels  29 us (20%)
  starting transfers between devices  15.3 us (10%)
  local copies, waits for them, and re-layouts  11.6 us (8%)
    ppermute x3, waiting for transfers between devices, on_device(): parts[d] = lax.ppermute(chunk(d), 'tm', ring('tm', d))  43 us
    all_to_all x3, blocking collectives, a2a(): return lax.all_to_all(v, axis, 0, 0, tiled=True)  38.8 us
    pallas_call x1, Pallas kernels, factors(): pl.pallas_call(functools.partial(factor_kernel, widths), out_shape=jax.Sh...  20 us
    unnamed x18, local copies, waits for them, and re-layouts  7.54 us
    pallas_call x1, Pallas kernels, grams(): pl.pallas_call(gram_kernel, out_shape=(jax.ShapeDtypeStruct((8 * r, k), j...  6.37 us
    ppermute x3, starting transfers between devices, on_device(): parts[d] = lax.ppermute(chunk(d), 'tm', ring('tm', d))  5.81 us
    ppermute x3, waiting for transfers between devices, on_device(): back[d] = lax.ppermute(share(d), 'tm', ring('tm', d))  5.71 us
    ppermute x1, starting transfers between devices, sum_everywhere(): other = lax.ppermute(v, 'core', ring('core', 1))  4.5 us
  transfers between devices with their start and end apart: 8, of which 7 were waited for; matrix products, arithmetic and copies ran while one was open for 0% of the time, Pallas kernels for 0%

profile of v1, /device:TPU:1, one launch (start us, length us, event | category | flops | bytes accessed | tf_op | source)
XLA Modules:
  0.0 145.5 jit_solution(3610481505302279608)
XLA Ops:
  0.0 3.9 %constant_dynamic-slice_fusion = (f32[128,2048]{1,0:T(8,128)}, f32[128,2048]{1,0:T(8,128)}, f32[128,2048]{1,0:T(8,128)S(1)}, f32[128,2048]{1,0:T(8,128)}) fusion(f32[128,8192]{1,0:T(8,128)} %param.3, s32[]{:T(128)S(6)} %select_n.86, s32[]{:T(128)S(6)} %select_n.82, s32[]{:T(128)S(6)} %select_n.80, s32[]{:T(128)S(6)} %select_n.84), kind=kLoop, calls=%fused_computation.9 | loop fusion | bytes 8388624 | tf_op jit(solution)/shard_map/dynamic_slice | solution.py:268
  3.9 2.1 %collective-permute-start = (f32[128,2048]{1,0:T(8,128)}, f32[128,2048]{1,0:T(8,128)S(1)}, u32[]{:S(2)}, u32[]{:S(2)}) collective-permute-start(f32[128,2048]{1,0:T(8,128)} %get-tuple-element.12), channel_id=1, source_target_pairs={{0,1},{1,2},{2,3},{3,0},{4,5},{5,6},{6,7},{7,4},{8,9},{9,10},{10,1... | collective-permute-start | bytes 3145736 | tf_op jit(solution)/shard_map/ppermute | solution.py:272
  6.1 2.6 %collective-permute-start.1 = (f32[128,2048]{1,0:T(8,128)}, f32[128,2048]{1,0:T(8,128)S(1)}, u32[]{:S(2)}, u32[]{:S(2)}) collective-permute-start(f32[128,2048]{1,0:T(8,128)} %get-tuple-element.14), channel_id=1, source_target_pairs={{0,2},{1,3},{2,0},{3,1},{4,6},{5,7},{6,4},{7,5},{8,10},{9,11},{10,... | collective-permute-start | bytes 3145736 | tf_op jit(solution)/shard_map/ppermute | solution.py:272
  8.7 1.1 collective-permute-start.2
  9.7 0.1 copy.12
  9.9 0.1 copy.14
  9.9 18.6 %collective-permute-done.p1 = f32[128,2048]{1,0:T(8,128)S(1)} collective-permute-done((f32[128,2048]{1,0:T(8,128)}, f32[128,2048]{1,0:T(8,128)S(1)}, u32[]{:S(2)}, u32[]{:S(2)}) %collective-permute-start) | collective-permute-done | bytes 1048608 | tf_op jit(solution)/shard_map/ppermute | solution.py:272
  28.5 1.0 copy-done.2
  29.5 24.4 %collective-permute-done.1.p2 = f32[128,2048]{1,0:T(8,128)S(1)} collective-permute-done((f32[128,2048]{1,0:T(8,128)}, f32[128,2048]{1,0:T(8,128)S(1)}, u32[]{:S(2)}, u32[]{:S(2)}) %collective-permute-start.1) | collective-permute-done | bytes 1048608 | tf_op jit(solution)/shard_map/ppermute | solution.py:272
  53.9 1.0 copy-done.4
  54.9 1.2 copy-done.3
  56.1 1.2 copy-done.5
  57.3 6.4 %grams.1 = (f32[512,128]{1,0:T(8,128)S(1)}, bf16[512,2048]{1,0:T(8,128)(2,1)S(1)}, bf16[512,2048]{1,0:T(8,128)(2,1)S(1)}) custom-call(s32[4]{0:T(128)S(1)} %and_select_fusion.order_ref, f32[128,64]{1,0:T(8,128)S(1)} %bitcast.26, f32[64,128]{1,0:T(8,128)S(1)} %bitcast.28, f32[128,2048]{1,0:T(8,128)S(1)} %get-tuple-element.13.p0, f32[128,2048]{1,0:T(8,128)S(1)} %copy-done.3, ...), custom_call_target="tpu_custom_call" | custom-call | tf_op jit(solution)/shard_map/grams/pallas_call | solution.py:178
  63.7 1.3 copy-done
  65.1 1.6 %collective-permute-start.3 = (f32[256,128]{1,0:T(8,128)S(1)}, f32[256,128]{1,0:T(8,128)S(1)}, u32[]{:S(2)}, u32[]{:S(2)}) collective-permute-start(f32[256,128]{1,0:T(8,128)S(1)} %dynamic-slice_bitcast_fusion.4), channel_id=1, source_target_pairs={{0,4},{4,0},{1,5},{5,1},{2,6},{6,2},{3,7},{7,3},{8,12},{12,8},{9,1... | collective-permute-start | bytes 393224 | tf_op jit(solution)/shard_map/ppermute | solution.py:250
  66.7 1.0 collective-permute-done.3
  67.7 15.9 %all_to_all.15 = f32[8,32,128]{2,1,0:T(8,128)S(1)} all-to-all(f32[8,32,128]{2,1,0:T(8,128)S(1)} %bitcast.34), channel_id=1, replica_groups=mesh['z'=8,'x'=4,'core'=2,'tm'=4] {'z'}, dimensions={0} | all-to-all | bytes 262144 | tf_op jit(solution)/shard_map/all_to_all | solution.py:236
  83.6 12.5 %all_to_all.16 = f32[16,32,128]{2,1,0:T(8,128)S(1)} all-to-all(f32[16,32,128]{2,1,0:T(8,128)S(1)} %broadcast_in_dim.4), channel_id=1, replica_groups=mesh['z'=8,'x'=4,'core'=2,'tm'=4] {'x','tm'}, dimensions={0} | all-to-all | bytes 524288 | tf_op jit(solution)/shard_map/all_to_all | solution.py:236
  96.2 10.4 %all_to_all.17 = f32[8,32,128]{2,1,0:T(8,128)S(1)} all-to-all(f32[8,32,128]{2,1,0:T(8,128)S(1)} %broadcast_in_dim.5), channel_id=1, replica_groups=mesh['z'=8,'x'=4,'core'=2,'tm'=4] {'z'}, dimensions={0} | all-to-all | bytes 262144 | tf_op jit(solution)/shard_map/all_to_all | solution.py:236
  106.6 4.5 %collective-permute-start.4 = (f32[256,128]{1,0:T(8,128)S(1)}, f32[256,128]{1,0:T(8,128)S(1)}, u32[]{:S(2)}, u32[]{:S(2)}) collective-permute-start(f32[256,128]{1,0:T(8,128)S(1)} %bitcast.33), channel_id=1, source_target_pairs={{0,4},{4,0},{1,5},{5,1},{2,6},{6,2},{3,7},{7,3},{8,12},{12,8},{9,1... | collective-permute-start | bytes 393224 | tf_op jit(solution)/shard_map/ppermute | solution.py:255
  111.1 0.1 copy.15.merge_ref
  111.2 0.9 collective-permute-done.4
  112.2 20.0 %factors.1.coef_ref = f32[64,512]{1,0:T(8,128)S(1)} custom-call(f32[512,128]{1,0:T(8,128)S(1)} %pad_maximum_fusion.red_ref, f32[128,64]{1,0:T(8,128)S(1)} %bitcast.27, f32[64,128]{1,0:T(8,128)S(1)} %bitcast.29, f32[128,64]{1,0:T(8,128)S(1)} %copy.15.merge_ref, f32[64,128]{1,0:T(8,128)S(1)} %bitcast.32), custom_call_target="tpu_custom_call" | custom-call | tf_op jit(solution)/shard_map/factors/pallas_call | solution.py:123
  132.2 1.6 %copy-done.1 = bf16[512,2048]{1,0:T(8,128)(2,1)S(1)} copy-done((bf16[512,2048]{1,0:T(8,128)(2,1)S(1)}, bf16[512,2048]{1,0:T(8,128)(2,1)}, u32[]{:S(2)}) %copy-start.1) | copy-done | bytes 2097176
  133.8 1.2 modes.1
  135.1 0.2 collective-permute-start.5
  135.3 1.8 %collective-permute-start.6 = (f32[16,2048]{1,0:T(8,128)S(1)}, f32[16,2048]{1,0:T(8,128)S(1)}, u32[]{:S(2)}, u32[]{:S(2)}) collective-permute-start(f32[16,2048]{1,0:T(8,128)S(1)} %get-tuple-element.16), channel_id=1, source_target_pairs={{0,2},{1,3},{2,0},{3,1},{4,6},{5,7},{6,4},{7,5},{8,10},{9,11},{10,... | collective-permute-start | bytes 393224 | tf_op jit(solution)/shard_map/ppermute | solution.py:283
  137.1 1.4 collective-permute-start.7
  138.4 3.4 %collective-permute-done.5.p1 = f32[16,2048]{1,0:T(8,128)S(1)} collective-permute-done((f32[16,2048]{1,0:T(8,128)S(1)}, f32[16,2048]{1,0:T(8,128)S(1)}, u32[]{:S(2)}, u32[]{:S(2)}) %collective-permute-start.5) | collective-permute-done | bytes 131104 | tf_op jit(solution)/shard_map/ppermute | solution.py:283
  141.8 1.4 collective-permute-done.6.p2
  143.2 1.0 collective-permute-done.7.p3
  144.1 1.4 place.1
  (22 shorter events, 0.2 us)
Async XLA Ops:
  0.0 9.7 %copy-start.7 = (f32[128,64]{0,1:T(8,128)S(1)}, f32[128,64]{0,1:T(8,128)}, u32[]{:S(2)}) copy-start(f32[128,64]{0,1:T(8,128)} %param.4) | copy-start | bytes 98308
  3.9 107.2 %copy-start.6 = (f32[128,64]{0,1:T(8,128)S(1)}, f32[128,64]{0,1:T(8,128)}, u32[]{:S(2)}) copy-start(f32[128,64]{0,1:T(8,128)} %param.5) | copy-start | bytes 98308
  3.9 24.6 %collective-permute-start = (f32[128,2048]{1,0:T(8,128)}, f32[128,2048]{1,0:T(8,128)S(1)}, u32[]{:S(2)}, u32[]{:S(2)}) collective-permute-start(f32[128,2048]{1,0:T(8,128)} %get-tuple-element.12), channel_id=1, source_target_pairs={{0,1},{1,2},{2,3},{3,0},{4,5},{5,6},{6,7},{7,4},{8,9},{9,10},{10,1... | collective-permute-start | bytes 3145736 | tf_op jit(solution)/shard_map/ppermute | solution.py:272
  6.1 47.9 %collective-permute-start.1 = (f32[128,2048]{1,0:T(8,128)}, f32[128,2048]{1,0:T(8,128)S(1)}, u32[]{:S(2)}, u32[]{:S(2)}) collective-permute-start(f32[128,2048]{1,0:T(8,128)} %get-tuple-element.14), channel_id=1, source_target_pairs={{0,2},{1,3},{2,0},{3,1},{4,6},{5,7},{6,4},{7,5},{8,10},{9,11},{10,... | collective-permute-start | bytes 3145736 | tf_op jit(solution)/shard_map/ppermute | solution.py:272
  8.7 46.2 %collective-permute-start.2 = (f32[128,2048]{1,0:T(8,128)}, f32[128,2048]{1,0:T(8,128)}, u32[]{:S(2)}, u32[]{:S(2)}) collective-permute-start(f32[128,2048]{1,0:T(8,128)} %get-tuple-element.11), channel_id=1, source_target_pairs={{0,3},{1,0},{2,1},{3,2},{4,7},{5,4},{6,5},{7,6},{8,11},{9,8},{10,9... | collective-permute-start | bytes 3145736 | tf_op jit(solution)/shard_map/ppermute | solution.py:272
  28.5 1.0 copy-start.2
  53.9 1.0 copy-start.4
  54.9 1.2 copy-start.3
  56.1 1.2 copy-start.5
  63.7 1.4 copy-start
  65.1 2.6 %collective-permute-start.3 = (f32[256,128]{1,0:T(8,128)S(1)}, f32[256,128]{1,0:T(8,128)S(1)}, u32[]{:S(2)}, u32[]{:S(2)}) collective-permute-start(f32[256,128]{1,0:T(8,128)S(1)} %dynamic-slice_bitcast_fusion.4), channel_id=1, source_target_pairs={{0,4},{4,0},{1,5},{5,1},{2,6},{6,2},{3,7},{7,3},{8,12},{12,8},{9,1... | collective-permute-start | bytes 393224 | tf_op jit(solution)/shard_map/ppermute | solution.py:250
  106.6 5.5 %collective-permute-start.4 = (f32[256,128]{1,0:T(8,128)S(1)}, f32[256,128]{1,0:T(8,128)S(1)}, u32[]{:S(2)}, u32[]{:S(2)}) collective-permute-start(f32[256,128]{1,0:T(8,128)S(1)} %bitcast.33), channel_id=1, source_target_pairs={{0,4},{4,0},{1,5},{5,1},{2,6},{6,2},{3,7},{7,3},{8,12},{12,8},{9,1... | collective-permute-start | bytes 393224 | tf_op jit(solution)/shard_map/ppermute | solution.py:255
  132.2 1.6 %copy-start.1 = (bf16[512,2048]{1,0:T(8,128)(2,1)S(1)}, bf16[512,2048]{1,0:T(8,128)(2,1)}, u32[]{:S(2)}) copy-start(bf16[512,2048]{1,0:T(8,128)(2,1)} %copy-done) | copy-start | bytes 6291460
  135.1 6.7 %collective-permute-start.5 = (f32[16,2048]{1,0:T(8,128)S(1)}, f32[16,2048]{1,0:T(8,128)S(1)}, u32[]{:S(2)}, u32[]{:S(2)}) collective-permute-start(f32[16,2048]{1,0:T(8,128)S(1)} %get-tuple-element.17), channel_id=1, source_target_pairs={{0,1},{1,2},{2,3},{3,0},{4,5},{5,6},{6,7},{7,4},{8,9},{9,10},{10,1... | collective-permute-start | bytes 393224 | tf_op jit(solution)/shard_map/ppermute | solution.py:283
  135.3 7.9 %collective-permute-start.6 = (f32[16,2048]{1,0:T(8,128)S(1)}, f32[16,2048]{1,0:T(8,128)S(1)}, u32[]{:S(2)}, u32[]{:S(2)}) collective-permute-start(f32[16,2048]{1,0:T(8,128)S(1)} %get-tuple-element.16), channel_id=1, source_target_pairs={{0,2},{1,3},{2,0},{3,1},{4,6},{5,7},{6,4},{7,5},{8,10},{9,11},{10,... | collective-permute-start | bytes 393224 | tf_op jit(solution)/shard_map/ppermute | solution.py:283
  137.1 7.1 %collective-permute-start.7 = (f32[16,2048]{1,0:T(8,128)S(1)}, f32[16,2048]{1,0:T(8,128)S(1)}, u32[]{:S(2)}, u32[]{:S(2)}) collective-permute-start(f32[16,2048]{1,0:T(8,128)S(1)} %get-tuple-element.15), channel_id=1, source_target_pairs={{0,3},{1,0},{2,1},{3,2},{4,7},{5,4},{6,5},{7,6},{8,11},{9,8},{10,9... | collective-permute-start | bytes 393224 | tf_op jit(solution)/shard_map/ppermute | solution.py:283

commit v2 on v0

v2 whole, which is shorter than its diff:
```python
import functools

import jax
import jax.numpy as jnp
from jax import lax
from jax.experimental import pallas as pl
from jax.experimental.pallas import tpu as pltpu
from jax.sharding import Mesh, PartitionSpec as P

HI = lax.Precision.HIGHEST
SUB = 8
VMEM = pl.BlockSpec(memory_space=pltpu.VMEM)
ANY = pl.BlockSpec(memory_space=pl.ANY)
SPACE = ("z", "x", "core")
PARAMS = pltpu.CompilerParams(vmem_limit_bytes=56 * 2**20)
CHUNKS = (512, 512, 512, 512)
PLAN = (((16, True), (16, True)), ((8, False), (16, False)), ((16, False), (16, False)))


def mm(a, b):
    return jnp.dot(a, b, precision=HI, preferred_element_type=jnp.float32)


def mmt(a, b):
    return lax.dot_general(a, b, (((1,), (1,)), ((), ())), precision=HI, preferred_element_type=jnp.float32)


def mtm(a, b):
    return lax.dot_general(a, b, (((0,), (0,)), ((), ())), precision=HI, preferred_element_type=jnp.float32)


def eliminate(mats, width, product, packed=False):
    n, lanes = mats[0].shape
    count = n // SUB
    rows = lax.broadcasted_iota(jnp.int32, (SUB, lanes), 0)
    left = lax.broadcasted_iota(jnp.int32, (SUB, lanes), 1) < n
    work = [[m[b * SUB : (b + 1) * SUB, :] for b in range(count)] for m in mats]

    def row(v, c):
        return jnp.broadcast_to(v[c : c + 1, :], (SUB, lanes))

    def column(v, c):
        wide = jnp.broadcast_to(v[:, c : c + 1], (SUB, lanes))
        if not packed:
            return wide
        return jnp.where(left, wide, jnp.broadcast_to(v[:, n + c : n + c + 1], (SUB, lanes)))

    for first in range(0, n, width):
        lo, hi = first // SUB, (first + width + SUB - 1) // SUB
        end = hi if product else count
        spread = [
            [{b: column(w[b], first + c) for b in range((first + c) // SUB, end)} for c in range(width)] for w in work
        ]
        pivots = [[] for _ in mats]
        for c in range(width):
            p, at = divmod(first + c, SUB)
            for w, t, d in zip(work, spread, pivots):
                d.append(row(t[c][p], at))
                inverse = 1.0 / d[c]
                pivot_row = row(w[p], at) * inverse
                for later in range(c + 1, width):
                    lp, lat = divmod(first + later, SUB)
                    scale = row(t[c][lp], lat) * inverse
                    for b in range(lp, end):
                        t[later][b] = t[later][b] - t[c][b] * scale
                w[p] = w[p] - jnp.where(rows > at, t[c][p], 0.0) * pivot_row
                for b in range(p + 1, end):
                    w[b] = w[b] - t[c][b] * pivot_row
        for w, d in zip(work, pivots):
            for b in range(lo, hi):
                scale = d[(b - lo) * SUB]
                for at in range(1, SUB):
                    scale = jnp.where(rows >= at, d[(b - lo) * SUB + at], scale)
                w[b] = w[b] * lax.rsqrt(scale)
            if product and hi < count:
                top = jnp.concatenate(w[lo:hi], 0)
                if packed:
                    below = jnp.concatenate([mtm(top[:, :n], top[:, :n]), mtm(top[:, n:], top[:, n:])], 1)
                else:
                    below = mtm(top[:, :n], top)
                for b in range(hi, count):
                    w[b] = w[b] - below[b * SUB : (b + 1) * SUB, :]
    return [jnp.concatenate(w, 0) for w in work]


def factor(sketched, grams, plan):
    r = sketched[0].shape[0]
    row = lax.broadcasted_iota(jnp.int32, (r, r), 0)
    lane = lax.broadcasted_iota(jnp.int32, (r, r), 1)
    eye = (row == lane).astype(jnp.float32)
    whole = eliminate([jnp.concatenate([s, eye], 1) for s in sketched], *plan[0])
    inverse = [e[:, r:] for e in whole]
    mixed = [mm(i, b) for i, b in zip(inverse, grams)]
    inner = [mmt(m, m) for m in mixed]
    if len(inner) > 1:
        both = [jnp.concatenate(inner[i : i + 2], 1) for i in range(0, len(inner), 2)]
        both = eliminate(both, *plan[1], packed=True)
        upper = [half for e in both for half in (e[:, :r], e[:, r:])]
    else:
        upper = eliminate(inner, *plan[1])
    return inverse, [jnp.where(lane >= row, u, 0.0) for u in upper]


def stack_pair(upper, maps, cross, sketch):
    ua, ub = upper
    r = ua.shape[0]
    va, vb = mtm(sketch[:r, :], ua), mtm(sketch[r:, :], ub)
    ta, tb = va + mmt(vb, cross), vb + mm(va, cross)
    sketched = mmt(ta, va) + mmt(tb, vb)
    gram = jnp.concatenate([mmt(ta, ua), mmt(tb, ub)], 1)
    return sketched, gram, jnp.concatenate([mm(va, maps[0]), mm(vb, maps[1])], 1)


def combine(red_ref, wl, wm):
    r = wl.shape[1]
    grams = [red_ref[w * r : (w + 1) * r, :] for w in range(4)]
    z, u = factor([mm(g, wl) for g in grams], grams, PLAN[0])
    pairs = []
    for i in range(2):
        cross = mmt(mm(z[2 * i], red_ref[4 * r : 5 * r, i * r : (i + 1) * r]), z[2 * i + 1])
        pairs.append(stack_pair(u[2 * i : 2 * i + 2], z[2 * i : 2 * i + 2], cross, wm))
    inverse, u = factor([p[0] for p in pairs], [p[1] for p in pairs], PLAN[1])
    z = [mm(i, p[2]) for i, p in zip(inverse, pairs)]
    cross = mmt(mm(z[0], red_ref[5 * r : 7 * r, :]), z[1])
    sketched, gram, rows = stack_pair(u, z, cross, wm)
    inverse, u = factor([sketched], [gram], PLAN[2])
    z = mm(inverse[0], rows)
    return u[0], jnp.concatenate([mmt(z[:, w * r : (w + 1) * r], wl) for w in range(4)], 1)


def dot_rows(a, b):
    return lax.dot_general(a, b, (((1,), (1,)), ((), ())), preferred_element_type=jnp.float32)


def split(x):
    high = x.astype(jnp.bfloat16)
    return high, (x - high.astype(jnp.float32)).astype(jnp.bfloat16)


def in_window_order(leaf_ref):
    k = leaf_ref.shape[0]
    return jnp.concatenate([leaf_ref[pl.ds(j, k // 4, stride=4), :] for j in range(4)], 0)


def cut_kernel(base, archive_ref, o1, o2, o3, sem):
    t = lax.axis_index("tm")
    cells = archive_ref.shape[1] // 4
    copies = []
    for d, out in enumerate((o1, o2, o3)):
        at = pl.multiple_of(lax.rem(t + d + 1, 4) * cells + base, 128)
        copies.append(pltpu.make_async_copy(archive_ref.at[:, pl.ds(at, out.shape[1])], out, sem.at[d]))
    for copy in copies:
        copy.start()
    for copy in copies:
        copy.wait()


def cut(archive, base, step):
    return pl.pallas_call(
        functools.partial(cut_kernel, base),
        out_shape=(jax.ShapeDtypeStruct((archive.shape[0], step), jnp.float32),) * 3,
        in_specs=[ANY],
        out_specs=(ANY,) * 3,
        scratch_shapes=[pltpu.SemaphoreType.DMA((3,))],
        compiler_params=PARAMS,
        name="cut",
    )(archive)


def gram_kernel(base, first, last, leaf_ref, archive_ref, p1, p2, p3, *refs):
    sofar, refs = refs[: not first], refs[not first :]
    sums, (high_out, low_out, held, high_ref, low_ref, red, sem) = refs[: 1 + last], refs[1 + last :]
    t = lax.axis_index("tm")
    step = held.shape[2]
    mine = pl.multiple_of(t * (archive_ref.shape[1] // 4) + base, 128)
    sources = (archive_ref.at[:, pl.ds(mine, step)], p1, p2, p3)
    copies = [pltpu.make_async_copy(p, held.at[d], sem.at[d]) for d, p in enumerate(sources)]
    for copy in copies:
        copy.start()
    for d, copy in enumerate(copies):
        copy.wait()
        per = held.shape[1] // 4
        for w in range(4):
            at = pl.ds(pl.multiple_of(w * 4 * per + lax.rem(t + 4 - d, 4) * per, per), per)
            high, low = split(held[d, w * per : (w + 1) * per, :])
            high_ref[at, :] = high
            low_ref[at, :] = low
    outward = [pltpu.make_async_copy(high_ref, high_out, sem.at[4]), pltpu.make_async_copy(low_ref, low_out, sem.at[5])]
    for copy in outward:
        copy.start()
    k, r = leaf_ref.shape
    halves = [(ref[: 2 * k, :], ref[2 * k :, :]) for ref in (high_ref, low_ref)]

    def block(index, i, j):
        hi, li, hj, lj = halves[0][i], halves[1][i], halves[0][j], halves[1][j]
        g = dot_rows(hi, hj) + (dot_rows(hi, lj) + dot_rows(li, hj) + dot_rows(li, lj))
        return g if first else sofar[0][index * 2 * k : (index + 1) * 2 * k, :] + g

    blocks = [block(index, i, j) for index, (i, j) in enumerate(((0, 0), (1, 1), (0, 1)))]
    if last:
        wl = in_window_order(leaf_ref)
        blank = jnp.zeros_like(wl)
        wide = jnp.concatenate([jnp.concatenate([wl, blank], 1), jnp.concatenate([blank, wl], 1)], 0)
        own = [mtm(wide, g) for g in blocks]
        for w in range(4):
            red[w * r : (w + 1) * r, :] = own[w // 2][w % 2 * r : (w % 2 + 1) * r, w % 2 * k : (w % 2 + 1) * k]
        beside = mm(jnp.concatenate([own[0][:r, k:], own[1][:r, k:]], 0), wl)
        red[4 * r : 5 * r, :] = jnp.concatenate([beside[:r], beside[r:]], 1)
        red[5 * r : 7 * r, :] = mm(own[2], wide)
        red[7 * r :, :] = jnp.zeros((r, k), jnp.float32)
        core = lax.axis_index("core")
        half = 4 * r
        sums[0][...] = red[pl.ds(pl.multiple_of(core * half, half), half), :]
        sums[1][...] = red[pl.ds(pl.multiple_of((1 - core) * half, half), half), :]
    else:
        for index, g in enumerate(blocks):
            sums[0][index * 2 * k : (index + 1) * 2 * k, :] = g
    for copy in outward:
        copy.wait()


def grams(base, leaf, archive, parts, sofar, last):
    k, r = leaf.shape
    rows, step = parts[0].shape
    halves = (jax.ShapeDtypeStruct((4 * k, step), jnp.bfloat16),) * 2
    if last:
        sums = (jax.ShapeDtypeStruct((4 * r, k), jnp.float32),) * 2
    else:
        sums = (jax.ShapeDtypeStruct((6 * k, 2 * k), jnp.float32),)
    return pl.pallas_call(
        functools.partial(gram_kernel, base, not sofar, last),
        out_shape=sums + halves,
        in_specs=[VMEM] + [ANY] * 4 + [VMEM] * len(sofar),
        out_specs=(VMEM,) * len(sums) + (ANY,) * 2,
        scratch_shapes=[
            pltpu.VMEM((4, rows, step), jnp.float32),
            pltpu.VMEM((4 * k, step), jnp.bfloat16),
            pltpu.VMEM((4 * k, step), jnp.bfloat16),
            pltpu.VMEM((8 * r, k), jnp.float32),
            pltpu.SemaphoreType.DMA((6,)),
        ],
        compiler_params=PARAMS,
        name="grams",
    )(leaf, archive, *parts, *sofar)


def modes_kernel(count, mine_ref, other_ref, leaf_ref, merge_ref, *refs):
    sources, outs, (red, held, total, sem) = refs[: 2 * count], refs[2 * count : -4], refs[-4:]
    copies, at = [], [0, 0]
    for i, s in enumerate(sources):
        side = i // count
        copies.append(pltpu.make_async_copy(s, held.at[side, :, pl.ds(at[side], s.shape[1])], sem.at[i]))
        at[side] += s.shape[1]
    for copy in copies:
        copy.start()
    core = lax.axis_index("core")
    half = mine_ref.shape[0]
    red[pl.ds(pl.multiple_of(core * half, half), half), :] = mine_ref[...]
    red[pl.ds(pl.multiple_of((1 - core) * half, half), half), :] = other_ref[...]
    scale, rows = combine(red, in_window_order(leaf_ref), merge_ref[...])
    high, low = split(rows)

    def dot(a, b):
        return jnp.dot(a, b, preferred_element_type=jnp.float32)

    for copy in copies:
        copy.wait()
    basis = dot(high, held[0]) + (dot(high, held[1]) + dot(low, held[0]))
    total[...] = mm(scale, basis)
    t = lax.axis_index("tm")
    per = outs[0].shape[0]
    for d, out in enumerate(outs):
        out[...] = total[pl.ds(pl.multiple_of(lax.rem(t + d, 4) * per, per), per), :]


def modes(mine, other, leaf, merge, high, low):
    k, r = leaf.shape
    count, cells = len(high), sum(h.shape[1] for h in high)
    return pl.pallas_call(
        functools.partial(modes_kernel, count),
        out_shape=(jax.ShapeDtypeStruct((r // 4, cells), jnp.float32),) * 4,
        in_specs=[VMEM] * 4 + [ANY] * (2 * count),
        out_specs=(VMEM,) * 4,
        scratch_shapes=[
            pltpu.VMEM((8 * r, k), jnp.float32),
            pltpu.VMEM((2, 4 * k, cells), jnp.bfloat16),
            pltpu.VMEM((r, cells), jnp.float32),
            pltpu.SemaphoreType.DMA((2 * count,)),
        ],
        compiler_params=PARAMS,
        name="modes",
    )(mine, other, leaf, merge, *high, *low)


def ring(axis, step):
    n = lax.axis_size(axis)
    return [(i, (i + step) % n) for i in range(n)]


def a2a(v, axis):
    return lax.all_to_all(v, axis, 0, 0, tiled=True)


def spread_over(v, axis):
    n = lax.axis_size(axis)
    return a2a(jnp.broadcast_to(v[None], (n, *v.shape)), axis)


def sum_everywhere(mine, theirs):
    rows, lanes = mine.shape
    n = lax.axis_size("z")
    v = mine + lax.ppermute(theirs, "core", ring("core", 1))
    v = a2a(v.reshape(n, rows // n, lanes), "z").sum(0)
    v = spread_over(v, ("x", "tm")).sum(0)
    v = spread_over(v, "z").reshape(rows, lanes)
    return v, lax.ppermute(v, "core", ring("core", 1))


def on_device(archive, leaf, merge):
    r = leaf.shape[1]
    n = lax.axis_size("tm")
    t = lax.axis_index("tm")
    cells = archive.shape[1] // n
    sends = (2, 1, 3)
    bases = [sum(CHUNKS[:c]) for c in range(len(CHUNKS))]
    moved = []
    for base, step in zip(bases, CHUNKS):
        pieces = cut(archive, base, step)
        moved.append({d: lax.ppermute(pieces[d - 1], "tm", ring("tm", d)) for d in sends})
    sums, high, low = [], [], []
    for c, (base, parts) in enumerate(zip(bases, moved)):
        *sums, h, l = grams(base, leaf, archive, [parts[d] for d in (1, 2, 3)], sums, c == len(CHUNKS) - 1)
        high.append(h)
        low.append(l)
    out = modes(*sum_everywhere(*sums), leaf, merge, high, low)
    back = {d: lax.ppermute(out[d], "tm", ring("tm", d)) for d in sends}
    whole = lax.dynamic_update_slice_in_dim(jnp.zeros((r // n, n * cells), jnp.float32), out[0], t * cells, 1)
    for d in sends:
        whole = lax.dynamic_update_slice_in_dim(whole, back[d], (t + n - d) % n * cells, 1)
    return whole


def solution(mesh):
    fine = Mesh(mesh.devices.reshape(mesh.devices.shape[0] // 8, 4, 2, 4), (*SPACE, "tm"))
    return jax.shard_map(
        on_device, mesh=fine, in_specs=(P("tm", SPACE), P(), P()), out_specs=P("tm", SPACE), check_vma=False
    )
```

time: 1750 us -> 223 us (0.13)
  blocking collectives: 1490 us -> 39.7 us
  Pallas kernels: 0 us -> 139 us
  waiting for transfers between devices: 131 us -> 9.3 us
  other arithmetic: 59.7 us -> 0.96 us
  matrix products: 48.2 us -> 0 us
  starting transfers between devices: 6.34 us -> 27.1 us
    psum x6 -> x0, blocking collectives: 1490 us -> none  [sum_cells(): return lax.psum(matrix, 'space')]
    pallas_call x0 -> x9, Pallas kernels: none -> 139 us  [the longest x4 99.8 us: cut(): pl.pallas_call(functools.partial(cut_kernel, base), out_shape=(jax.ShapeD...]
    ppermute x2 -> x17, waiting for transfers between devices: 83.8 us -> 9.3 us  [the longest x3 5.06 us: on_device(): back = {d: lax.ppermute(out[d], 'tm', ring('tm', d)) for d in sends}]
    another operation x24 -> x0, other arithmetic: 55.8 us -> none  [the longest x9 19.6 us: merge_piece(): lower_y = jnp.linalg.cholesky(reduce_fn(contract(sketched, sketched)))]
    all_to_all x1 -> x0, waiting for transfers between devices: 47 us -> none  [on_device(): lax.all_to_all(parted, 'tm', split_axis=0, concat_axis=0, tiled=True)]
    dot_general x15 -> x0, matrix products: 42.4 us -> none  [the longest x9 21 us: contract(): lax.dot_general(former, latter, (((1,), (1,)), ((), ())), precision=lax.P...]
    all_to_all x0 -> x3, blocking collectives: none -> 39.7 us  [a2a(): return lax.all_to_all(v, axis, 0, 0, tiled=True)]
    ppermute x2 -> x17, starting transfers between devices: 1.19 us -> 27.1 us  [the longest x12 16 us: on_device(): lax.ppermute(pieces[d - 1], 'tm', ring('tm', d))]
  transfers between devices with their start and end apart: 3 -> 17, of which waited for: 3 -> 5; matrix products, arithmetic and copies ran while one was open for 0% -> 1% of each run, Pallas kernels for 0% -> 40%
where the time goes in v2:
time: 223 us
  Pallas kernels  139 us (62%)
  blocking collectives  39.7 us (18%)
  starting transfers between devices  27.1 us (12%)
  waiting for transfers between devices  9.3 us (4%)
  local copies, waits for them, and re-layouts  6.05 us (3%)
    pallas_call x4, Pallas kernels, cut(): pl.pallas_call(functools.partial(cut_kernel, base), out_shape=(jax.ShapeD...  99.8 us
    all_to_all x3, blocking collectives, a2a(): return lax.all_to_all(v, axis, 0, 0, tiled=True)  39.7 us
    pallas_call x1, Pallas kernels, modes(): pl.pallas_call(functools.partial(modes_kernel, count), out_shape=(jax.Sha...  20.9 us
    pallas_call x4, Pallas kernels, grams(): pl.pallas_call(functools.partial(gram_kernel, base, not sofar, last), out...  18.5 us
    ppermute x12, starting transfers between devices, on_device(): lax.ppermute(pieces[d - 1], 'tm', ring('tm', d))  16 us
    ppermute x3, waiting for transfers between devices, on_device(): back = {d: lax.ppermute(out[d], 'tm', ring('tm', d)) for d in sends}  5.06 us
    ppermute x1, starting transfers between devices, sum_everywhere(): return (v, lax.ppermute(v, 'core', ring('core', 1)))  4.5 us
  transfers between devices with their start and end apart: 17, of which 5 were waited for; matrix products, arithmetic and copies ran while one was open for 1% of the time, Pallas kernels for 40%

profile of v2, /device:TPU:1, one launch (start us, length us, event | category | flops | bytes accessed | tf_op | source)
XLA Modules:
  0.0 222.6 jit_solution(3819003680864234437)
XLA Ops:
  0.0 24.9 %cut.7 = (f32[128,512]{1,0:T(8,128)}, f32[128,512]{1,0:T(8,128)}, f32[128,512]{1,0:T(8,128)}) custom-call(f32[128,8192]{1,0:T(8,128)} %archive_ref.15), custom_call_target="tpu_custom_call" | custom-call | tf_op jit(solution)/shard_map/cut/pallas_call | solution.py:159
  25.0 3.8 %collective-permute-start.10 = (f32[128,512]{1,0:T(8,128)}, f32[128,512]{1,0:T(8,128)S(1)}, u32[]{:S(2)}, u32[]{:S(2)}) collective-permute-start(f32[128,512]{1,0:T(8,128)} %get-tuple-element.44), channel_id=1, source_target_pairs={{0,2},{1,3},{2,0},{3,1},{4,6},{5,7},{6,4},{7,5},{8,10},{9,11},{10,... | collective-permute-start | bytes 786440 | tf_op jit(solution)/shard_map/ppermute | solution.py:329
  28.8 0.8 collective-permute-start.11
  30.3 24.9 %cut.6 = (f32[128,512]{1,0:T(8,128)}, f32[128,512]{1,0:T(8,128)}, f32[128,512]{1,0:T(8,128)}) custom-call(f32[128,8192]{1,0:T(8,128)} %archive_ref.15), custom_call_target="tpu_custom_call" | custom-call | tf_op jit(solution)/shard_map/cut/pallas_call | solution.py:159
  55.7 2.8 %collective-permute-start.7 = (f32[128,512]{1,0:T(8,128)}, f32[128,512]{1,0:T(8,128)S(1)}, u32[]{:S(2)}, u32[]{:S(2)}) collective-permute-start(f32[128,512]{1,0:T(8,128)} %get-tuple-element.41), channel_id=1, source_target_pairs={{0,2},{1,3},{2,0},{3,1},{4,6},{5,7},{6,4},{7,5},{8,10},{9,11},{10,... | collective-permute-start | bytes 786440 | tf_op jit(solution)/shard_map/ppermute | solution.py:329
  58.5 24.9 %cut.5 = (f32[128,512]{1,0:T(8,128)}, f32[128,512]{1,0:T(8,128)}, f32[128,512]{1,0:T(8,128)}) custom-call(f32[128,8192]{1,0:T(8,128)} %archive_ref.15), custom_call_target="tpu_custom_call" | custom-call | tf_op jit(solution)/shard_map/cut/pallas_call | solution.py:159
  83.6 1.4 collective-permute-start.3
  85.0 24.9 %cut.4 = (f32[128,512]{1,0:T(8,128)}, f32[128,512]{1,0:T(8,128)}, f32[128,512]{1,0:T(8,128)}) custom-call(f32[128,8192]{1,0:T(8,128)} %archive_ref.15), custom_call_target="tpu_custom_call" | custom-call | tf_op jit(solution)/shard_map/cut/pallas_call | solution.py:159
  110.5 2.1 collective-permute-start.5
  112.7 1.9 collective-permute-start.1
  114.6 1.3 collective-permute-start.2
  115.9 0.7 copy.13.leaf_ref
  116.7 4.2 %grams.4 = (f32[768,256]{1,0:T(8,128)}, bf16[512,512]{1,0:T(8,128)(2,1)}, bf16[512,512]{1,0:T(8,128)(2,1)}) custom-call(f32[128,64]{1,0:T(8,128)} %copy.13.leaf_ref, f32[128,8192]{1,0:T(8,128)} %archive_ref.15, f32[128,512]{1,0:T(8,128)} %copy-done.4, f32[128,512]{1,0:T(8,128)} %copy-done.2, f32[128,512]{1,0:T(8,128)} %copy-done.3), custom_call_target="tpu_custom_call" | custom-call | tf_op jit(solution)/shard_map/grams/pallas_call | solution.py:230
  120.9 4.6 %grams.5 = (f32[768,256]{1,0:T(8,128)}, bf16[512,512]{1,0:T(8,128)(2,1)}, bf16[512,512]{1,0:T(8,128)(2,1)}) custom-call(f32[128,64]{1,0:T(8,128)} %copy.13.leaf_ref, f32[128,8192]{1,0:T(8,128)} %archive_ref.15, f32[128,512]{1,0:T(8,128)} %copy-done.5, f32[128,512]{1,0:T(8,128)} %copy-done.6, f32[128,512]{1,0:T(8,128)} %copy-done.8, ...), custom_call_target="tpu_custom_call" | custom-call | tf_op jit(solution)/shard_map/grams/pallas_call | solution.py:230
  126.4 4.6 %grams.6 = (f32[768,256]{1,0:T(8,128)}, bf16[512,512]{1,0:T(8,128)(2,1)}, bf16[512,512]{1,0:T(8,128)(2,1)}) custom-call(f32[128,64]{1,0:T(8,128)} %copy.13.leaf_ref, f32[128,8192]{1,0:T(8,128)} %archive_ref.15, f32[128,512]{1,0:T(8,128)} %copy-done.7, f32[128,512]{1,0:T(8,128)} %copy-done.10, f32[128,512]{1,0:T(8,128)} %copy-done.12, ...), custom_call_target="tpu_custom_call" | custom-call | tf_op jit(solution)/shard_map/grams/pallas_call | solution.py:230
  131.1 2.7 %collective-permute-done.2.p3 = f32[128,512]{1,0:T(8,128)S(1)} collective-permute-done((f32[128,512]{1,0:T(8,128)}, f32[128,512]{1,0:T(8,128)S(1)}, u32[]{:S(2)}, u32[]{:S(2)}) %collective-permute-start.2) | collective-permute-done | bytes 262176 | tf_op jit(solution)/shard_map/ppermute | solution.py:329
  134.5 5.1 %grams.7 = (f32[256,128]{1,0:T(8,128)}, f32[256,128]{1,0:T(8,128)}, bf16[512,512]{1,0:T(8,128)(2,1)}, bf16[512,512]{1,0:T(8,128)(2,1)}) custom-call(f32[128,64]{1,0:T(8,128)} %copy.13.leaf_ref, f32[128,8192]{1,0:T(8,128)} %archive_ref.15, f32[128,512]{1,0:T(8,128)} %copy-done.9, f32[128,512]{1,0:T(8,128)} %copy-done.11, f32[128,512]{1,0:T(8,128)} %copy-done.13, ...), custom_call_target="tpu_custom_call" | custom-call | tf_op jit(solution)/shard_map/grams/pallas_call | solution.py:230
  139.6 2.6 %collective-permute-start.12 = (f32[256,128]{1,0:T(8,128)}, f32[256,128]{1,0:T(8,128)S(1)}, u32[]{:S(2)}, u32[]{:S(2)}) collective-permute-start(f32[256,128]{1,0:T(8,128)} %get-tuple-element.50), channel_id=1, source_target_pairs={{0,4},{4,0},{1,5},{5,1},{2,6},{6,2},{3,7},{7,3},{8,12},{12,8},{9,1... | collective-permute-start | bytes 393224 | tf_op jit(solution)/shard_map/ppermute | solution.py:312
  142.2 1.2 collective-permute-done.12
  143.4 0.9 add.37
  144.3 15.9 %all_to_all.15 = f32[8,32,128]{2,1,0:T(8,128)S(1)} all-to-all(f32[8,32,128]{2,1,0:T(8,128)S(1)} %bitcast.4), channel_id=1, replica_groups=mesh['z'=8,'x'=4,'core'=2,'tm'=4] {'z'}, dimensions={0} | all-to-all | bytes 262144 | tf_op jit(solution)/shard_map/all_to_all | solution.py:301
  160.2 13.4 %all_to_all.16 = f32[16,32,128]{2,1,0:T(8,128)S(1)} all-to-all(f32[16,32,128]{2,1,0:T(8,128)S(1)} %broadcast_in_dim.7), channel_id=1, replica_groups=mesh['z'=8,'x'=4,'core'=2,'tm'=4] {'x','tm'}, dimensions={0} | all-to-all | bytes 524288 | tf_op jit(solution)/shard_map/all_to_all | solution.py:301
  173.7 10.4 %all_to_all.17 = f32[8,32,128]{2,1,0:T(8,128)S(1)} all-to-all(f32[8,32,128]{2,1,0:T(8,128)S(1)} %broadcast_in_dim.8), channel_id=1, replica_groups=mesh['z'=8,'x'=4,'core'=2,'tm'=4] {'z'}, dimensions={0} | all-to-all | bytes 262144 | tf_op jit(solution)/shard_map/all_to_all | solution.py:301
  184.1 4.5 %collective-permute-start.13 = (f32[256,128]{1,0:T(8,128)S(1)}, f32[256,128]{1,0:T(8,128)S(1)}, u32[]{:S(2)}, u32[]{:S(2)}) collective-permute-start(f32[256,128]{1,0:T(8,128)S(1)} %bitcast.2), channel_id=1, source_target_pairs={{0,4},{4,0},{1,5},{5,1},{2,6},{6,2},{3,7},{7,3},{8,12},{12,8},{9,1... | collective-permute-start | bytes 393224 | tf_op jit(solution)/shard_map/ppermute | solution.py:316
  188.6 0.7 copy.15.merge_ref
  190.2 20.9 %modes.1 = (f32[16,2048]{1,0:T(8,128)}, f32[16,2048]{1,0:T(8,128)}, f32[16,2048]{1,0:T(8,128)}, f32[16,2048]{1,0:T(8,128)}) custom-call(f32[256,128]{1,0:T(8,128)} %bitcast.3, f32[256,128]{1,0:T(8,128)} %copy-done.14, f32[128,64]{1,0:T(8,128)} %copy.13.leaf_ref, f32[128,64]{1,0:T(8,128)} %copy.15.merge_ref, bf16[512,512]{1,0:T(8,128)(2,1)} %get-tuple-element.51.refs_0_, ...), custom_call_target="tpu_custom_call" | custom-call | tf_op jit(solution)/shard_map/modes/pallas_call | solution.py:279
  211.1 1.3 collective-permute-start.14
  212.6 2.6 %collective-permute-start.16 = (f32[16,2048]{1,0:T(8,128)}, f32[16,2048]{1,0:T(8,128)S(1)}, u32[]{:S(2)}, u32[]{:S(2)}) collective-permute-start(f32[16,2048]{1,0:T(8,128)} %get-tuple-element.62), channel_id=1, source_target_pairs={{0,3},{1,0},{2,1},{3,2},{4,7},{5,4},{6,5},{7,6},{8,11},{9,8},{10,9... | collective-permute-start | bytes 393224 | tf_op jit(solution)/shard_map/ppermute | solution.py:336
  215.2 0.9 constant_dynamic-update-slice_fusion.3
  216.1 1.6 collective-permute-done.14
  217.7 3.5 %collective-permute-done.15 = f32[16,2048]{1,0:T(8,128)S(1)} collective-permute-done((f32[16,2048]{1,0:T(8,128)}, f32[16,2048]{1,0:T(8,128)S(1)}, u32[]{:S(2)}, u32[]{:S(2)}) %collective-permute-start.15) | collective-permute-done | bytes 131104 | tf_op jit(solution)/shard_map/ppermute | solution.py:336
  221.2 0.8 copy-done.1
  (64 shorter events, 5.1 us)
Async XLA Ops:
  25.0 58.5 %collective-permute-start.10 = (f32[128,512]{1,0:T(8,128)}, f32[128,512]{1,0:T(8,128)S(1)}, u32[]{:S(2)}, u32[]{:S(2)}) collective-permute-start(f32[128,512]{1,0:T(8,128)} %get-tuple-element.44), channel_id=1, source_target_pairs={{0,2},{1,3},{2,0},{3,1},{4,6},{5,7},{6,4},{7,5},{8,10},{9,11},{10,... | collective-permute-start | bytes 786440 | tf_op jit(solution)/shard_map/ppermute | solution.py:329
  28.8 54.8 %collective-permute-start.11 = (f32[128,512]{1,0:T(8,128)}, f32[128,512]{1,0:T(8,128)S(1)}, u32[]{:S(2)}, u32[]{:S(2)}) collective-permute-start(f32[128,512]{1,0:T(8,128)} %get-tuple-element.45), channel_id=1, source_target_pairs={{0,3},{1,0},{2,1},{3,2},{4,7},{5,4},{6,5},{7,6},{8,11},{9,8},{10,9... | collective-permute-start | bytes 786440 | tf_op jit(solution)/shard_map/ppermute | solution.py:329
  29.6 80.4 %collective-permute-start.9 = (f32[128,512]{1,0:T(8,128)}, f32[128,512]{1,0:T(8,128)S(1)}, u32[]{:S(2)}, u32[]{:S(2)}) collective-permute-start(f32[128,512]{1,0:T(8,128)} %get-tuple-element.43), channel_id=1, source_target_pairs={{0,1},{1,2},{2,3},{3,0},{4,5},{5,6},{6,7},{7,4},{8,9},{9,10},{10,1... | collective-permute-start | bytes 786440 | tf_op jit(solution)/shard_map/ppermute | solution.py:329
  55.2 28.2 %copy-start.18 = (f32[128,512]{1,0:T(8,128)S(1)}, f32[128,512]{1,0:T(8,128)}, u32[]{:S(2)}) copy-start(f32[128,512]{1,0:T(8,128)} %get-tuple-element.42) | copy-start | bytes 786436
  55.2 55.3 %collective-permute-start.6 = (f32[128,512]{1,0:T(8,128)}, f32[128,512]{1,0:T(8,128)S(1)}, u32[]{:S(2)}, u32[]{:S(2)}) collective-permute-start(f32[128,512]{1,0:T(8,128)} %get-tuple-element.40), channel_id=1, source_target_pairs={{0,1},{1,2},{2,3},{3,0},{4,5},{5,6},{6,7},{7,4},{8,9},{9,10},{10,1... | collective-permute-start | bytes 786440 | tf_op jit(solution)/shard_map/ppermute | solution.py:329
  55.7 60.2 %copy-start.15 = (f32[128,64]{0,1:T(8,128)S(1)}, f32[128,64]{0,1:T(8,128)}, u32[]{:S(2)}) copy-start(f32[128,64]{0,1:T(8,128)} %param.4) | copy-start | bytes 98308
  55.7 56.9 %collective-permute-start.7 = (f32[128,512]{1,0:T(8,128)}, f32[128,512]{1,0:T(8,128)S(1)}, u32[]{:S(2)}, u32[]{:S(2)}) collective-permute-start(f32[128,512]{1,0:T(8,128)} %get-tuple-element.41), channel_id=1, source_target_pairs={{0,2},{1,3},{2,0},{3,1},{4,6},{5,7},{6,4},{7,5},{8,10},{9,11},{10,... | collective-permute-start | bytes 786440 | tf_op jit(solution)/shard_map/ppermute | solution.py:329
  83.4 27.1 %copy-start.17 = (f32[128,512]{1,0:T(8,128)S(1)}, f32[128,512]{1,0:T(8,128)}, u32[]{:S(2)}) copy-start(f32[128,512]{1,0:T(8,128)} %get-tuple-element.39) | copy-start | bytes 786436
  83.4 33.2 %copy-start.2 = (f32[128,512]{1,0:T(8,128)}, f32[128,512]{1,0:T(8,128)S(1)}, u32[]{:S(2)}) copy-start(f32[128,512]{1,0:T(8,128)S(1)} %collective-permute-done.10.p2) | copy-start | bytes 786436
  83.5 29.2 %collective-permute-start.8 = (f32[128,512]{1,0:T(8,128)S(1)}, f32[128,512]{1,0:T(8,128)S(1)}, u32[]{:S(2)}, u32[]{:S(2)}) collective-permute-start(f32[128,512]{1,0:T(8,128)S(1)} %copy-done.18), channel_id=1, source_target_pairs={{0,3},{1,0},{2,1},{3,2},{4,7},{5,4},{6,5},{7,6},{8,11},{9,8},{10,9... | collective-permute-start | bytes 786440 | tf_op jit(solution)/shard_map/ppermute | solution.py:329
  83.6 33.1 %copy-start.3 = (f32[128,512]{1,0:T(8,128)}, f32[128,512]{1,0:T(8,128)S(1)}, u32[]{:S(2)}) copy-start(f32[128,512]{1,0:T(8,128)S(1)} %collective-permute-done.11.p3) | copy-start | bytes 786436
  83.6 31.0 %collective-permute-start.3 = (f32[128,512]{1,0:T(8,128)}, f32[128,512]{1,0:T(8,128)S(1)}, u32[]{:S(2)}, u32[]{:S(2)}) collective-permute-start(f32[128,512]{1,0:T(8,128)} %get-tuple-element.37), channel_id=1, source_target_pairs={{0,1},{1,2},{2,3},{3,0},{4,5},{5,6},{6,7},{7,4},{8,9},{9,10},{10,1... | collective-permute-start | bytes 786440 | tf_op jit(solution)/shard_map/ppermute | solution.py:329
  110.0 6.7 %copy-start.4 = (f32[128,512]{1,0:T(8,128)}, f32[128,512]{1,0:T(8,128)S(1)}, u32[]{:S(2)}) copy-start(f32[128,512]{1,0:T(8,128)S(1)} %collective-permute-done.9.p1) | copy-start | bytes 786436
  110.0 15.6 %collective-permute-start.4 = (f32[128,512]{1,0:T(8,128)}, f32[128,512]{1,0:T(8,128)S(1)}, u32[]{:S(2)}, u32[]{:S(2)}) collective-permute-start(f32[128,512]{1,0:T(8,128)} %get-tuple-element.38), channel_id=1, source_target_pairs={{0,2},{1,3},{2,0},{3,1},{4,6},{5,7},{6,4},{7,5},{8,10},{9,11},{10,... | collective-permute-start | bytes 786440 | tf_op jit(solution)/shard_map/ppermute | solution.py:329
  110.5 10.4 %copy-start.5 = (f32[128,512]{1,0:T(8,128)}, f32[128,512]{1,0:T(8,128)S(1)}, u32[]{:S(2)}) copy-start(f32[128,512]{1,0:T(8,128)S(1)} %collective-permute-done.6.p1) | copy-start | bytes 786436
  110.5 15.1 %collective-permute-start.5 = (f32[128,512]{1,0:T(8,128)S(1)}, f32[128,512]{1,0:T(8,128)S(1)}, u32[]{:S(2)}, u32[]{:S(2)}) collective-permute-start(f32[128,512]{1,0:T(8,128)S(1)} %copy-done.17), channel_id=1, source_target_pairs={{0,3},{1,0},{2,1},{3,2},{4,7},{5,4},{6,5},{7,6},{8,11},{9,8},{10,9... | collective-permute-start | bytes 786440 | tf_op jit(solution)/shard_map/ppermute | solution.py:329
  112.6 8.3 %copy-start.6 = (f32[128,512]{1,0:T(8,128)}, f32[128,512]{1,0:T(8,128)S(1)}, u32[]{:S(2)}) copy-start(f32[128,512]{1,0:T(8,128)S(1)} %collective-permute-done.7.p2) | copy-start | bytes 786436
  112.6 18.4 %collective-permute-start = (f32[128,512]{1,0:T(8,128)}, f32[128,512]{1,0:T(8,128)S(1)}, u32[]{:S(2)}, u32[]{:S(2)}) collective-permute-start(f32[128,512]{1,0:T(8,128)} %get-tuple-element.34), channel_id=1, source_target_pairs={{0,1},{1,2},{2,3},{3,0},{4,5},{5,6},{6,7},{7,4},{8,9},{9,10},{10,1... | collective-permute-start | bytes 786440 | tf_op jit(solution)/shard_map/ppermute | solution.py:329
  112.7 8.3 %copy-start.8 = (f32[128,512]{1,0:T(8,128)}, f32[128,512]{1,0:T(8,128)S(1)}, u32[]{:S(2)}) copy-start(f32[128,512]{1,0:T(8,128)S(1)} %collective-permute-done.8.p3) | copy-start | bytes 786436
  112.7 18.4 %collective-permute-start.1 = (f32[128,512]{1,0:T(8,128)}, f32[128,512]{1,0:T(8,128)S(1)}, u32[]{:S(2)}, u32[]{:S(2)}) collective-permute-start(f32[128,512]{1,0:T(8,128)} %get-tuple-element.35), channel_id=1, source_target_pairs={{0,2},{1,3},{2,0},{3,1},{4,6},{5,7},{6,4},{7,5},{8,10},{9,11},{10,... | collective-permute-start | bytes 786440 | tf_op jit(solution)/shard_map/ppermute | solution.py:329
  114.6 10.9 %copy-start.7 = (f32[128,512]{1,0:T(8,128)}, f32[128,512]{1,0:T(8,128)S(1)}, u32[]{:S(2)}) copy-start(f32[128,512]{1,0:T(8,128)S(1)} %collective-permute-done.3.p1) | copy-start | bytes 786436
  114.6 19.2 %collective-permute-start.2 = (f32[128,512]{1,0:T(8,128)}, f32[128,512]{1,0:T(8,128)S(1)}, u32[]{:S(2)}, u32[]{:S(2)}) collective-permute-start(f32[128,512]{1,0:T(8,128)} %get-tuple-element.36), channel_id=1, source_target_pairs={{0,3},{1,0},{2,1},{3,2},{4,7},{5,4},{6,5},{7,6},{8,11},{9,8},{10,9... | collective-permute-start | bytes 786440 | tf_op jit(solution)/shard_map/ppermute | solution.py:329
  131.0 57.6 %copy-start.16 = (f32[128,64]{0,1:T(8,128)S(1)}, f32[128,64]{0,1:T(8,128)}, u32[]{:S(2)}) copy-start(f32[128,64]{0,1:T(8,128)} %param.5) | copy-start | bytes 98308
  131.0 2.8 %copy-start.9 = (f32[128,512]{1,0:T(8,128)}, f32[128,512]{1,0:T(8,128)S(1)}, u32[]{:S(2)}) copy-start(f32[128,512]{1,0:T(8,128)S(1)} %collective-permute-done.p1) | copy-start | bytes 786436
  131.0 2.8 %copy-start.11 = (f32[128,512]{1,0:T(8,128)}, f32[128,512]{1,0:T(8,128)S(1)}, u32[]{:S(2)}) copy-start(f32[128,512]{1,0:T(8,128)S(1)} %collective-permute-done.1.p2) | copy-start | bytes 786436
  139.6 3.8 %collective-permute-start.12 = (f32[256,128]{1,0:T(8,128)}, f32[256,128]{1,0:T(8,128)S(1)}, u32[]{:S(2)}, u32[]{:S(2)}) collective-permute-start(f32[256,128]{1,0:T(8,128)} %get-tuple-element.50), channel_id=1, source_target_pairs={{0,4},{4,0},{1,5},{5,1},{2,6},{6,2},{3,7},{7,3},{8,12},{12,8},{9,1... | collective-permute-start | bytes 393224 | tf_op jit(solution)/shard_map/ppermute | solution.py:312
  184.1 5.5 %copy-start = (f32[8,32,128]{2,1,0:T(8,128)}, f32[8,32,128]{2,1,0:T(8,128)S(1)}, u32[]{:S(2)}) copy-start(f32[8,32,128]{2,1,0:T(8,128)S(1)} %all_to_all.17) | copy-start | bytes 393220
  184.1 5.5 %collective-permute-start.13 = (f32[256,128]{1,0:T(8,128)S(1)}, f32[256,128]{1,0:T(8,128)S(1)}, u32[]{:S(2)}, u32[]{:S(2)}) collective-permute-start(f32[256,128]{1,0:T(8,128)S(1)} %bitcast.2), channel_id=1, source_target_pairs={{0,4},{4,0},{1,5},{5,1},{2,6},{6,2},{3,7},{7,3},{8,12},{12,8},{9,1... | collective-permute-start | bytes 393224 | tf_op jit(solution)/shard_map/ppermute | solution.py:316
  211.1 6.5 %collective-permute-start.14 = (f32[16,2048]{1,0:T(8,128)}, f32[16,2048]{1,0:T(8,128)S(1)}, u32[]{:S(2)}, u32[]{:S(2)}) collective-permute-start(f32[16,2048]{1,0:T(8,128)} %get-tuple-element.60), channel_id=1, source_target_pairs={{0,2},{1,3},{2,0},{3,1},{4,6},{5,7},{6,4},{7,5},{8,10},{9,11},{10,... | collective-permute-start | bytes 393224 | tf_op jit(solution)/shard_map/ppermute | solution.py:336
  212.5 8.7 %collective-permute-start.15 = (f32[16,2048]{1,0:T(8,128)}, f32[16,2048]{1,0:T(8,128)S(1)}, u32[]{:S(2)}, u32[]{:S(2)}) collective-permute-start(f32[16,2048]{1,0:T(8,128)} %get-tuple-element.61), channel_id=1, source_target_pairs={{0,1},{1,2},{2,3},{3,0},{4,5},{5,6},{6,7},{7,4},{8,9},{9,10},{10,1... | collective-permute-start | bytes 393224 | tf_op jit(solution)/shard_map/ppermute | solution.py:336
  212.6 8.6 %collective-permute-start.16 = (f32[16,2048]{1,0:T(8,128)}, f32[16,2048]{1,0:T(8,128)S(1)}, u32[]{:S(2)}, u32[]{:S(2)}) collective-permute-start(f32[16,2048]{1,0:T(8,128)} %get-tuple-element.62), channel_id=1, source_target_pairs={{0,3},{1,0},{2,1},{3,2},{4,7},{5,4},{6,5},{7,6},{8,11},{9,8},{10,9... | collective-permute-start | bytes 393224 | tf_op jit(solution)/shard_map/ppermute | solution.py:336
  221.2 0.8 copy-start.1
  (4 other events, 2.8 us)

commit v3 on v2

v3 whole, which is shorter than its diff:
```python
import functools

import jax
import jax.numpy as jnp
from jax import lax
from jax.experimental import pallas as pl
from jax.experimental.pallas import tpu as pltpu
from jax.sharding import Mesh, PartitionSpec as P

HI = lax.Precision.HIGHEST
SUB = 8
VMEM = pl.BlockSpec(memory_space=pltpu.VMEM)
ANY = pl.BlockSpec(memory_space=pl.ANY)
in_space = pltpu.with_memory_space_constraint
SPACE = ("z", "x", "core")
PARAMS = pltpu.CompilerParams(vmem_limit_bytes=12 * 2**20)
CHUNKS = (512, 512, 640, 384)
PLAN = (((16, True), (16, True)), ((8, False), (16, False)), ((16, False), (16, False)))


def mm(a, b):
    return jnp.dot(a, b, precision=HI, preferred_element_type=jnp.float32)


def mmt(a, b):
    return lax.dot_general(a, b, (((1,), (1,)), ((), ())), precision=HI, preferred_element_type=jnp.float32)


def mtm(a, b):
    return lax.dot_general(a, b, (((0,), (0,)), ((), ())), precision=HI, preferred_element_type=jnp.float32)


def eliminate(mats, width, product, packed=False):
    n, lanes = mats[0].shape
    count = n // SUB
    rows = lax.broadcasted_iota(jnp.int32, (SUB, lanes), 0)
    left = lax.broadcasted_iota(jnp.int32, (SUB, lanes), 1) < n
    work = [[m[b * SUB : (b + 1) * SUB, :] for b in range(count)] for m in mats]

    def row(v, c):
        return jnp.broadcast_to(v[c : c + 1, :], (SUB, lanes))

    def column(v, c):
        wide = jnp.broadcast_to(v[:, c : c + 1], (SUB, lanes))
        if not packed:
            return wide
        return jnp.where(left, wide, jnp.broadcast_to(v[:, n + c : n + c + 1], (SUB, lanes)))

    for first in range(0, n, width):
        lo, hi = first // SUB, (first + width + SUB - 1) // SUB
        end = hi if product else count
        spread = [
            [{b: column(w[b], first + c) for b in range((first + c) // SUB, end)} for c in range(width)] for w in work
        ]
        pivots = [[] for _ in mats]
        for c in range(width):
            p, at = divmod(first + c, SUB)
            for w, t, d in zip(work, spread, pivots):
                d.append(row(t[c][p], at))
                inverse = 1.0 / d[c]
                pivot_row = row(w[p], at) * inverse
                for later in range(c + 1, width):
                    lp, lat = divmod(first + later, SUB)
                    scale = row(t[c][lp], lat) * inverse
                    for b in range(lp, end):
                        t[later][b] = t[later][b] - t[c][b] * scale
                w[p] = w[p] - jnp.where(rows > at, t[c][p], 0.0) * pivot_row
                for b in range(p + 1, end):
                    w[b] = w[b] - t[c][b] * pivot_row
        for w, d in zip(work, pivots):
            for b in range(lo, hi):
                scale = d[(b - lo) * SUB]
                for at in range(1, SUB):
                    scale = jnp.where(rows >= at, d[(b - lo) * SUB + at], scale)
                w[b] = w[b] * lax.rsqrt(scale)
            if product and hi < count:
                top = jnp.concatenate(w[lo:hi], 0)
                if packed:
                    below = jnp.concatenate([mtm(top[:, :n], top[:, :n]), mtm(top[:, n:], top[:, n:])], 1)
                else:
                    below = mtm(top[:, :n], top)
                for b in range(hi, count):
                    w[b] = w[b] - below[b * SUB : (b + 1) * SUB, :]
    return [jnp.concatenate(w, 0) for w in work]


def factor(sketched, grams, plan):
    r = sketched[0].shape[0]
    row = lax.broadcasted_iota(jnp.int32, (r, r), 0)
    lane = lax.broadcasted_iota(jnp.int32, (r, r), 1)
    eye = (row == lane).astype(jnp.float32)
    whole = eliminate([jnp.concatenate([s, eye], 1) for s in sketched], *plan[0])
    inverse = [e[:, r:] for e in whole]
    mixed = [mm(i, b) for i, b in zip(inverse, grams)]
    inner = [mmt(m, m) for m in mixed]
    if len(inner) > 1:
        both = [jnp.concatenate(inner[i : i + 2], 1) for i in range(0, len(inner), 2)]
        both = eliminate(both, *plan[1], packed=True)
        upper = [half for e in both for half in (e[:, :r], e[:, r:])]
    else:
        upper = eliminate(inner, *plan[1])
    return inverse, [jnp.where(lane >= row, u, 0.0) for u in upper]


def stack_pair(upper, maps, cross, sketch_t):
    ua, ub = upper
    r = ua.shape[0]
    va, vb = mm(sketch_t[:, :r], ua), mm(sketch_t[:, r:], ub)
    ta, tb = va + mmt(vb, cross), vb + mm(va, cross)
    sketched = mmt(ta, va) + mmt(tb, vb)
    gram = jnp.concatenate([mmt(ta, ua), mmt(tb, ub)], 1)
    return sketched, gram, jnp.concatenate([mm(va, maps[0]), mm(vb, maps[1])], 1)


def combine(red_ref, wl, wmt):
    r = wl.shape[1]
    grams = [red_ref[w * r : (w + 1) * r, :] for w in range(4)]
    z, u = factor([mm(g, wl) for g in grams], grams, PLAN[0])
    pairs = []
    for i in range(2):
        cross = mmt(mm(z[2 * i], red_ref[4 * r : 5 * r, i * r : (i + 1) * r]), z[2 * i + 1])
        pairs.append(stack_pair(u[2 * i : 2 * i + 2], z[2 * i : 2 * i + 2], cross, wmt))
    inverse, u = factor([p[0] for p in pairs], [p[1] for p in pairs], PLAN[1])
    z = [mm(i, p[2]) for i, p in zip(inverse, pairs)]
    cross = mmt(mm(z[0], red_ref[5 * r : 7 * r, :]), z[1])
    sketched, gram, rows = stack_pair(u, z, cross, wmt)
    inverse, u = factor([sketched], [gram], PLAN[2])
    z = mm(inverse[0], rows)
    return u[0], jnp.concatenate([mmt(z[:, w * r : (w + 1) * r], wl) for w in range(4)], 1)


def dot_rows(a, b):
    return lax.dot_general(a, b, (((1,), (1,)), ((), ())), preferred_element_type=jnp.float32)


def split(x):
    high = x.astype(jnp.bfloat16)
    return high, (x - high.astype(jnp.float32)).astype(jnp.bfloat16)


def store_halves(t, d, rows_ref, high_ref, low_ref):
    per = rows_ref.shape[0] // 4
    for w in range(4):
        at = pl.ds(pl.multiple_of(w * 4 * per + lax.rem(t + 4 - d, 4) * per, per), per)
        high_ref[at, :], low_ref[at, :] = split(rows_ref[w * per : (w + 1) * per, :])


def own_cells(archive_ref, t, base, step):
    at = pl.multiple_of(t * (archive_ref.shape[1] // 4) + base, 128)
    return archive_ref.at[:, pl.ds(at, step)]


def gram_kernel(base, first, last, sketch_ref, archive_ref, p1, p2, p3, *refs):
    sofar, refs = refs[: not first], refs[not first :]
    sums, refs = refs[: 1 + last], refs[1 + last :]
    (high_ref, low_ref), refs = refs[:2], refs[2:]
    sketch_out, (held, red, sem, *turned) = refs[:first], refs[first:]
    t = lax.axis_index("tm")
    step = held.shape[2]
    sources = (own_cells(archive_ref, t, base, step), p1, p2, p3)
    copies = [pltpu.make_async_copy(p, held.at[d], sem.at[d]) for d, p in enumerate(sources)]
    for copy in copies:
        copy.start()
    if first:
        k = sketch_ref.shape[1]
        turned[0][...] = sketch_ref[...].T
        wl = jnp.concatenate([turned[0][pl.ds(j, k // 4, stride=4), :] for j in range(4)], 0)
        sketch_out[0][...] = wl
    else:
        wl = sketch_ref[...]
    k, r = wl.shape
    for d, copy in enumerate(copies):
        copy.wait()
        store_halves(t, d, held.at[d], high_ref, low_ref)
    halves = [(ref[: 2 * k, :], ref[2 * k :, :]) for ref in (high_ref, low_ref)]

    def block(i, j):
        hi, li, hj, lj = halves[0][i], halves[1][i], halves[0][j], halves[1][j]
        return dot_rows(hi, hj) + (dot_rows(hi, lj) + dot_rows(li, hj) + dot_rows(li, lj))

    blank = jnp.zeros_like(wl)
    wide = jnp.concatenate([jnp.concatenate([wl, blank], 1), jnp.concatenate([blank, wl], 1)], 0)
    own = [mtm(wide, block(i, j)) for i, j in ((0, 0), (1, 1), (0, 1))]

    def add(at, value):
        to = slice(at * r, at * r + value.shape[0])
        red[to, :] = value if first else sofar[0][to, :] + value

    for w in range(4):
        add(w, own[w // 2][w % 2 * r : (w % 2 + 1) * r, w % 2 * k : (w % 2 + 1) * k])
    beside = mm(jnp.concatenate([own[0][:r, k:], own[1][:r, k:]], 0), wl)
    add(4, jnp.concatenate([beside[:r], beside[r:]], 1))
    add(5, mm(own[2], wide))
    if first:
        red[7 * r :, :] = jnp.zeros((r, k), jnp.float32)
    else:
        red[7 * r :, :] = sofar[0][7 * r :, :]
    if last:
        core = lax.axis_index("core")
        half = 4 * r
        sums[0][...] = red[pl.ds(pl.multiple_of(core * half, half), half), :]
        sums[1][...] = red[pl.ds(pl.multiple_of((1 - core) * half, half), half), :]
    else:
        sums[0][...] = red[...]


def grams(base, sketch, archive, parts, sofar, last):
    first = not sofar
    k, r = max(sketch.shape), min(sketch.shape)
    rows, step = parts[0].shape
    halves = ((jax.ShapeDtypeStruct if first else pltpu.VMEM)((4 * k, step), jnp.bfloat16),) * 2
    sums = (jax.ShapeDtypeStruct((4 * r if last else 8 * r, k), jnp.float32),) * (1 + last)
    ordered = (jax.ShapeDtypeStruct((k, r), jnp.float32),) * first
    return pl.pallas_call(
        functools.partial(gram_kernel, base, first, last),
        out_shape=sums + halves + ordered,
        in_specs=[VMEM] + [ANY] * 4 + [VMEM] * len(sofar),
        out_specs=(VMEM,) * (len(sums) + 2 + first),
        scratch_shapes=[
            pltpu.VMEM((4, rows, step), jnp.float32),
            pltpu.VMEM((8 * r, k), jnp.float32),
            pltpu.SemaphoreType.DMA((4,)),
        ]
        + [pltpu.VMEM((k, r), jnp.float32)] * first,
        compiler_params=PARAMS,
        cost_estimate=pl.CostEstimate(flops=128 * k * k * step, bytes_accessed=48 * k * step, transcendentals=0),
        name="grams",
    )(sketch, in_space(archive, pltpu.HBM), *parts, *sofar)


def modes_kernel(count, mine_ref, other_ref, leaf_ref, merge_ref, *refs):
    highs, lows, outs, (red, total, early, sem) = refs[:count], refs[count : 2 * count], refs[2 * count : -4], refs[-4:]
    fetches = [pltpu.make_async_copy(s[0], early.at[i], sem.at[i]) for i, s in enumerate((highs, lows))]
    for fetch in fetches:
        fetch.start()
    t = lax.axis_index("tm")
    core = lax.axis_index("core")
    half = mine_ref.shape[0]
    red[pl.ds(pl.multiple_of(core * half, half), half), :] = mine_ref[...]
    red[pl.ds(pl.multiple_of((1 - core) * half, half), half), :] = other_ref[...]
    a, b = split(mm(*combine(red, leaf_ref[...], merge_ref[...])))

    def dot(a, b):
        return jnp.dot(a, b, preferred_element_type=jnp.float32)

    for fetch in fetches:
        fetch.wait()
    at = 0
    for high, low in zip((early.at[0], *highs[1:]), (early.at[1], *lows[1:])):
        step = high.shape[1]
        total[:, at : at + step] = dot(a, high[...]) + (dot(a, low[...]) + dot(b, high[...]))
        at += step
    per = outs[0].shape[0]
    for d, out in enumerate(outs):
        out[...] = total[pl.ds(pl.multiple_of(lax.rem(t + d, 4) * per, per), per), :]


def modes(mine, other, leaf, merge, high, low):
    k, r = leaf.shape
    count, cells = len(high), sum(h.shape[1] for h in high)
    return pl.pallas_call(
        functools.partial(modes_kernel, count),
        out_shape=(jax.ShapeDtypeStruct((r // 4, cells), jnp.float32),) * 4,
        in_specs=[VMEM] * 4 + ([ANY] + [VMEM] * (count - 1)) * 2,
        out_specs=(VMEM,) * 4,
        scratch_shapes=[
            pltpu.VMEM((8 * r, k), jnp.float32),
            pltpu.VMEM((r, cells), jnp.float32),
            pltpu.VMEM((2, *high[0].shape), jnp.bfloat16),
            pltpu.SemaphoreType.DMA((2,)),
        ],
        compiler_params=PARAMS,
        name="modes",
    )(mine, other, leaf, merge, *(in_space(v, pltpu.VMEM if i else pltpu.HBM) for s in (high, low) for i, v in enumerate(s)))


def place_kernel(p0, p1, p2, p3, out_ref, sem):
    t = lax.axis_index("tm")
    cells = p0.shape[1]
    copies = []
    for d, part in enumerate((p0, p1, p2, p3)):
        at = pl.multiple_of(lax.rem(t + 4 - d, 4) * cells, cells)
        copies.append(pltpu.make_async_copy(part, out_ref.at[:, pl.ds(at, cells)], sem.at[d]))
    for copy in copies:
        copy.start()
    for copy in copies:
        copy.wait()


def place(parts):
    rows, cells = parts[0].shape
    return pl.pallas_call(
        place_kernel,
        out_shape=jax.ShapeDtypeStruct((rows, 4 * cells), jnp.float32),
        in_specs=[ANY] * 4,
        out_specs=ANY,
        scratch_shapes=[pltpu.SemaphoreType.DMA((4,))],
        compiler_params=PARAMS,
        name="place",
    )(*parts)


def ring(axis, step):
    n = lax.axis_size(axis)
    return [(i, (i + step) % n) for i in range(n)]


def a2a(v, axis):
    return lax.all_to_all(v, axis, 0, 0, tiled=True)


def spread_over(v, axis):
    n = lax.axis_size(axis)
    return a2a(jnp.broadcast_to(v[None], (n, *v.shape)), axis)


def sum_everywhere(mine, theirs):
    rows, lanes = mine.shape
    n = lax.axis_size("z")
    v = mine + lax.ppermute(theirs, "core", ring("core", 1))
    v = a2a(v.reshape(n, rows // n, lanes), "z").sum(0)
    v = spread_over(v, ("x", "tm")).sum(0)
    v = spread_over(v, "z").reshape(rows, lanes)
    return v, lax.ppermute(v, "core", ring("core", 1))


def on_device(archive, leaf, merge):
    r = leaf.shape[1]
    n = lax.axis_size("tm")
    t = lax.axis_index("tm")
    cells = archive.shape[1] // n
    sends = (2, 1, 3)
    bases = [sum(CHUNKS[:c]) for c in range(len(CHUNKS))]
    last = len(CHUNKS) - 1

    def send(c, source):
        at = [(t + d) % n * cells + bases[c] for d in sends]
        pieces = [lax.dynamic_slice_in_dim(source, a, CHUNKS[c], 1) for a in at]
        arrived = {d: lax.ppermute(p, "tm", ring("tm", d)) for d, p in zip(sends, pieces)}
        return [arrived[d] for d in (1, 2, 3)]

    source = archive
    moved = [send(0, source)]
    source, marker = lax.optimization_barrier((source, leaf))
    moved.append(send(1, source))
    sums, high, low, sketch = [], [], [], marker.T
    for c in range(last):
        if c + 2 <= last:
            source, *moved[c] = lax.optimization_barrier((source, *moved[c]))
            moved.append(send(c + 2, source))
        if c == 0:
            total, h, l, sketch = grams(bases[c], sketch, archive, moved[c], sums, False)
        else:
            total, h, l = grams(bases[c], sketch, archive, moved[c], sums, False)
        source, total = lax.optimization_barrier((source, total))
        sums = [total]
        high.append(h)
        low.append(l)
    *sums, h, l = grams(bases[last], sketch, archive, moved[last], sums, True)
    out = modes(*sum_everywhere(*sums), sketch, merge.T, [*high, h], [*low, l])
    back = {d: lax.ppermute(out[d], "tm", ring("tm", d)) for d in sends}
    return place([out[0], *(back[d] for d in (1, 2, 3))])


def solution(mesh):
    fine = Mesh(mesh.devices.reshape(mesh.devices.shape[0] // 8, 4, 2, 4), (*SPACE, "tm"))
    return jax.shard_map(
        on_device, mesh=fine, in_specs=(P("tm", SPACE), P(), P()), out_specs=P("tm", SPACE), check_vma=False
    )
```

time: 223 us -> 131 us (0.59)
  Pallas kernels: 139 us -> 34.4 us
  waiting for transfers between devices: 9.3 us -> 20.7 us
    pallas_call x8 -> x5, Pallas kernels: 118 us -> 17.1 us  [the longest x4 16.3 us: grams(): pl.pallas_call(functools.partial(gram_kernel, base, first, last), out_sha...]
    ppermute x12, waiting for transfers between devices: 2.77 us -> 13 us  [send(): lax.ppermute(p, 'tm', ring('tm', d))]
    dynamic_slice x0 -> x4, local copies, waits for them, and re-layouts: none -> 6.17 us  [send(): pieces = [lax.dynamic_slice_in_dim(source, a, CHUNKS[c], 1) for a in at]]
    pallas_call x1, Pallas kernels: 20.9 us -> 17.3 us  [modes(): pl.pallas_call(functools.partial(modes_kernel, count), out_shape=(jax.Sha...]
    unnamed x40 -> x8, local copies, waits for them, and re-layouts: 4.37 us -> 1.61 us
  transfers between devices with their start and end apart: 17 -> 17, of which waited for: 5 -> 10; matrix products, arithmetic and copies ran while one was open for 1% -> 4% of each run, Pallas kernels for 40% -> 10%
where the time goes in v3:
time: 131 us; the launch traced here: 130 us
  blocking collectives  39.7 us (30%)
  Pallas kernels  34.4 us (26%)
  starting transfers between devices  27.3 us (21%)
  waiting for transfers between devices  20.7 us (16%)
  local copies, waits for them, and re-layouts  7.81 us (6%)
    all_to_all x3, blocking collectives, a2a(): return lax.all_to_all(v, axis, 0, 0, tiled=True)  39.7 us
    ppermute x12, starting transfers between devices, send(): lax.ppermute(p, 'tm', ring('tm', d))  17.8 us
    pallas_call x1, Pallas kernels, modes(): pl.pallas_call(functools.partial(modes_kernel, count), out_shape=(jax.Sha...  17.3 us
    pallas_call x4, Pallas kernels, grams(): pl.pallas_call(functools.partial(gram_kernel, base, first, last), out_sha...  16.3 us
    ppermute x12, waiting for transfers between devices, send(): lax.ppermute(p, 'tm', ring('tm', d))  13 us
    dynamic_slice x4, local copies, waits for them, and re-layouts, send(): pieces = [lax.dynamic_slice_in_dim(source, a, CHUNKS[c], 1) for a in at]  6.17 us
    ppermute x3, waiting for transfers between devices, on_device(): back = {d: lax.ppermute(out[d], 'tm', ring('tm', d)) for d in sends}  5.7 us
    ppermute x1, starting transfers between devices, sum_everywhere(): return (v, lax.ppermute(v, 'core', ring('core', 1)))  4.5 us
  transfers between devices with their start and end apart: 17, of which 10 were waited for; matrix products, arithmetic and copies ran while one was open for 4% of the time, Pallas kernels for 10%

profile of v3, /device:TPU:1, one launch (start us, length us, event | category | flops | bytes accessed | tf_op | source)
XLA Modules:
  0.0 130.3 jit_solution(6248772480383329553)
XLA Ops:
  0.0 1.2 constant_dynamic-slice_fusion.9
  1.2 2.2 %collective-permute-start = (f32[128,512]{1,0:T(8,128)S(1)}, f32[128,512]{1,0:T(8,128)S(1)}, u32[]{:S(2)}, u32[]{:S(2)}) collective-permute-start(f32[128,512]{1,0:T(8,128)S(1)} %get-tuple-element.78), channel_id=1, source_target_pairs={{0,1},{1,2},{2,3},{3,0},{4,5},{5,6},{6,7},{7,4},{8,9},{9,10},{10,1... | collective-permute-start | bytes 786440 | tf_op jit(solution)/shard_map/ppermute | solution.py:339
  3.4 2.6 %collective-permute-start.1 = (f32[128,512]{1,0:T(8,128)S(1)}, f32[128,512]{1,0:T(8,128)S(1)}, u32[]{:S(2)}, u32[]{:S(2)}) collective-permute-start(f32[128,512]{1,0:T(8,128)S(1)} %get-tuple-element.77), channel_id=1, source_target_pairs={{0,2},{1,3},{2,0},{3,1},{4,6},{5,7},{6,4},{7,5},{8,10},{9,11},{10,... | collective-permute-start | bytes 786440 | tf_op jit(solution)/shard_map/ppermute | solution.py:339
  6.0 1.1 collective-permute-start.2
  7.1 1.9 %constant_dynamic-slice_fusion.6 = (f32[128,512]{1,0:T(8,128)S(1)}, f32[128,512]{1,0:T(8,128)S(1)}, f32[128,512]{1,0:T(8,128)}) fusion(f32[128,8192]{1,0:T(8,128)} %archive_ref.7, s32[]{:T(128)S(6)} %select_n.77, s32[]{:T(128)S(6)} %select_n.76, s32[]{:T(128)S(6)} %select_n.75), kind=kLoop, calls=%fused_computation.6 | loop fusion | bytes 1572876 | tf_op jit(solution)/shard_map/dynamic_slice | solution.py:338
  10.1 1.9 %collective-permute-start.5 = (f32[128,512]{1,0:T(8,128)S(1)}, f32[128,512]{1,0:T(8,128)S(1)}, u32[]{:S(2)}, u32[]{:S(2)}) collective-permute-start(f32[128,512]{1,0:T(8,128)S(1)} %get-tuple-element.73), channel_id=1, source_target_pairs={{0,3},{1,0},{2,1},{3,2},{4,7},{5,4},{6,5},{7,6},{8,11},{9,8},{10,9... | collective-permute-start | bytes 786440 | tf_op jit(solution)/shard_map/ppermute | solution.py:339
  12.0 5.4 %collective-permute-done.1.p2 = f32[128,512]{1,0:T(8,128)S(1)} collective-permute-done((f32[128,512]{1,0:T(8,128)S(1)}, f32[128,512]{1,0:T(8,128)S(1)}, u32[]{:S(2)}, u32[]{:S(2)}) %collective-permute-start.1) | collective-permute-done | bytes 262176 | tf_op jit(solution)/shard_map/ppermute | solution.py:339
  17.4 1.0 collective-permute-done.2.p3
  18.4 2.0 %constant_dynamic-slice_fusion = (f32[128,640]{1,0:T(8,128)}, f32[128,640]{1,0:T(8,128)S(1)}, f32[128,640]{1,0:T(8,128)S(1)}) fusion(f32[128,8192]{1,0:T(8,128)} %archive_ref.7, s32[]{:T(128)S(6)} %select_n.83, s32[]{:T(128)S(6)} %select_n.82, s32[]{:T(128)S(6)} %select_n.81), kind=kLoop, calls=%fused_computation | loop fusion | bytes 1966092 | tf_op jit(solution)/shard_map/dynamic_slice | solution.py:338
  20.4 1.0 collective-permute-start.10
  21.3 2.9 %collective-permute-start.11 = (f32[128,640]{1,0:T(8,128)}, f32[128,640]{1,0:T(8,128)S(1)}, u32[]{:S(2)}, u32[]{:S(2)}) collective-permute-start(f32[128,640]{1,0:T(8,128)} %get-tuple-element.67), channel_id=1, source_target_pairs={{0,3},{1,0},{2,1},{3,2},{4,7},{5,4},{6,5},{7,6},{8,11},{9,8},{10,9... | collective-permute-start | bytes 983048 | tf_op jit(solution)/shard_map/ppermute | solution.py:339
  24.9 3.9 %grams.4 = (f32[512,128]{1,0:T(8,128)S(1)}, bf16[512,512]{1,0:T(8,128)(2,1)S(1)}, bf16[512,512]{1,0:T(8,128)(2,1)S(1)}, f32[128,64]{1,0:T(8,128)S(1)}) custom-call(f32[64,128]{1,0:T(8,128)S(1)} %bitcast.6, f32[128,8192]{1,0:T(8,128)} %archive_ref.7, f32[128,512]{1,0:T(8,128)S(1)} %collective-permute-done.p1, f32[128,512]{1,0:T(8,128)S(1)} %collective-permute-done.1.p2, ...), custom_call_target="tpu_custom_call" | custom-call | flops 1073741824 | bytes 3145728 | tf_op jit(solution)/shard_map/grams/pallas_call | solution.py:214
  30.4 1.2 constant_dynamic-slice_fusion.3
  31.5 1.5 %collective-permute-start.6 = (f32[128,384]{1,0:T(8,128)S(1)}, f32[128,384]{1,0:T(8,128)S(1)}, u32[]{:S(2)}, u32[]{:S(2)}) collective-permute-start(f32[128,384]{1,0:T(8,128)S(1)} %get-tuple-element.72), channel_id=1, source_target_pairs={{0,1},{1,2},{2,3},{3,0},{4,5},{5,6},{6,7},{7,4},{8,9},{9,10},{10,1... | collective-permute-start | bytes 589832 | tf_op jit(solution)/shard_map/ppermute | solution.py:339
  33.1 2.9 %collective-permute-start.7 = (f32[128,384]{1,0:T(8,128)S(1)}, f32[128,384]{1,0:T(8,128)S(1)}, u32[]{:S(2)}, u32[]{:S(2)}) collective-permute-start(f32[128,384]{1,0:T(8,128)S(1)} %get-tuple-element.71), channel_id=1, source_target_pairs={{0,2},{1,3},{2,0},{3,1},{4,6},{5,7},{6,4},{7,5},{8,10},{9,11},{10,... | collective-permute-start | bytes 589832 | tf_op jit(solution)/shard_map/ppermute | solution.py:339
  36.0 3.9 %grams.5 = (f32[512,128]{1,0:T(8,128)S(1)}, bf16[512,512]{1,0:T(8,128)(2,1)S(1)}, bf16[512,512]{1,0:T(8,128)(2,1)S(1)}) custom-call(f32[128,64]{1,0:T(8,128)S(1)} %get-tuple-element.41.sketch_ref.leaf_ref, f32[128,8192]{1,0:T(8,128)} %archive_ref.7, f32[128,512]{1,0:T(8,128)S(1)} %collective-permute-done.3.p1, f32[128,512]{1,0:T(8,128)S(1)} %collective-permute-done.4.p2, ...), custom_call_target="tpu_custom_call" | custom-call | flops 1073741824 | bytes 3145728 | tf_op jit(solution)/shard_map/grams/pallas_call | solution.py:214
  39.9 3.9 %collective-permute-done.11.p3 = f32[128,640]{1,0:T(8,128)S(1)} collective-permute-done((f32[128,640]{1,0:T(8,128)}, f32[128,640]{1,0:T(8,128)S(1)}, u32[]{:S(2)}, u32[]{:S(2)}) %collective-permute-start.11) | collective-permute-done | bytes 327712 | tf_op jit(solution)/shard_map/ppermute | solution.py:339
  43.7 4.6 %grams.6 = (f32[512,128]{1,0:T(8,128)S(1)}, bf16[512,640]{1,0:T(8,128)(2,1)S(1)}, bf16[512,640]{1,0:T(8,128)(2,1)S(1)}) custom-call(f32[128,64]{1,0:T(8,128)S(1)} %get-tuple-element.41.sketch_ref.leaf_ref, f32[128,8192]{1,0:T(8,128)} %archive_ref.7, f32[128,640]{1,0:T(8,128)S(1)} %collective-permute-done.9.p1, f32[128,640]{1,0:T(8,128)S(1)} %collective-permute-done.10.p2, ...), custom_call_target="tpu_custom_call" | custom-call | flops 1342177280 | bytes 3932160 | tf_op jit(solution)/shard_map/grams/pallas_call | solution.py:214
  48.9 2.2 %collective-permute-done.7.p2 = f32[128,384]{1,0:T(8,128)S(1)} collective-permute-done((f32[128,384]{1,0:T(8,128)S(1)}, f32[128,384]{1,0:T(8,128)S(1)}, u32[]{:S(2)}, u32[]{:S(2)}) %collective-permute-start.7) | collective-permute-done | bytes 196640 | tf_op jit(solution)/shard_map/ppermute | solution.py:339
  51.1 3.9 %grams.7 = (f32[256,128]{1,0:T(8,128)S(1)}, f32[256,128]{1,0:T(8,128)S(1)}, bf16[512,384]{1,0:T(8,128)(2,1)S(1)}, bf16[512,384]{1,0:T(8,128)(2,1)S(1)}) custom-call(f32[128,64]{1,0:T(8,128)S(1)} %get-tuple-element.41.sketch_ref.leaf_ref, f32[128,8192]{1,0:T(8,128)} %archive_ref.7, f32[128,384]{1,0:T(8,128)S(1)} %collective-permute-done.6.p1, ...), custom_call_target="tpu_custom_call" | custom-call | flops 805306368 | bytes 2359296 | tf_op jit(solution)/shard_map/grams/pallas_call | solution.py:214
  55.0 1.6 %collective-permute-start.12 = (f32[256,128]{1,0:T(8,128)S(1)}, f32[256,128]{1,0:T(8,128)S(1)}, u32[]{:S(2)}, u32[]{:S(2)}) collective-permute-start(f32[256,128]{1,0:T(8,128)S(1)} %get-tuple-element.54), channel_id=1, source_target_pairs={{0,4},{4,0},{1,5},{5,1},{2,6},{6,2},{3,7},{7,3},{8,12},{12,8},{9,1... | collective-permute-start | bytes 393224 | tf_op jit(solution)/shard_map/ppermute | solution.py:320
  56.7 1.0 collective-permute-done.12
  57.7 15.9 %all_to_all.15 = f32[8,32,128]{2,1,0:T(8,128)S(1)} all-to-all(f32[8,32,128]{2,1,0:T(8,128)S(1)} %bitcast.8), channel_id=1, replica_groups=mesh['z'=8,'x'=4,'core'=2,'tm'=4] {'z'}, dimensions={0} | all-to-all | bytes 262144 | tf_op jit(solution)/shard_map/all_to_all | solution.py:309
  73.6 13.4 %all_to_all.16 = f32[16,32,128]{2,1,0:T(8,128)S(1)} all-to-all(f32[16,32,128]{2,1,0:T(8,128)S(1)} %broadcast_in_dim.4), channel_id=1, replica_groups=mesh['z'=8,'x'=4,'core'=2,'tm'=4] {'x','tm'}, dimensions={0} | all-to-all | bytes 524288 | tf_op jit(solution)/shard_map/all_to_all | solution.py:309
  87.0 10.4 %all_to_all.17 = f32[8,32,128]{2,1,0:T(8,128)S(1)} all-to-all(f32[8,32,128]{2,1,0:T(8,128)S(1)} %broadcast_in_dim.5), channel_id=1, replica_groups=mesh['z'=8,'x'=4,'core'=2,'tm'=4] {'z'}, dimensions={0} | all-to-all | bytes 262144 | tf_op jit(solution)/shard_map/all_to_all | solution.py:309
  97.5 4.5 %collective-permute-start.13 = (f32[256,128]{1,0:T(8,128)S(1)}, f32[256,128]{1,0:T(8,128)S(1)}, u32[]{:S(2)}, u32[]{:S(2)}) collective-permute-start(f32[256,128]{1,0:T(8,128)S(1)} %bitcast.4), channel_id=1, source_target_pairs={{0,4},{4,0},{1,5},{5,1},{2,6},{6,2},{3,7},{7,3},{8,12},{12,8},{9,1... | collective-permute-start | bytes 393224 | tf_op jit(solution)/shard_map/ppermute | solution.py:324
  101.9 1.0 collective-permute-done.13.other_ref
  102.9 17.3 %modes.1 = (f32[16,2048]{1,0:T(8,128)S(1)}, f32[16,2048]{1,0:T(8,128)S(1)}, f32[16,2048]{1,0:T(8,128)S(1)}, f32[16,2048]{1,0:T(8,128)S(1)}) custom-call(f32[256,128]{1,0:T(8,128)S(1)} %bitcast.5, f32[256,128]{1,0:T(8,128)S(1)} %collective-permute-done.13.other_ref, f32[128,64]{1,0:T(8,128)S(1)} %get-tuple-element.41.sketch_ref.leaf_ref, ...), custom_call_target="tpu_custom_call" | custom-call | tf_op jit(solution)/shard_map/modes/pallas_call | solution.py:261
  120.5 1.8 %collective-permute-start.15 = (f32[16,2048]{1,0:T(8,128)S(1)}, f32[16,2048]{1,0:T(8,128)S(1)}, u32[]{:S(2)}, u32[]{:S(2)}) collective-permute-start(f32[16,2048]{1,0:T(8,128)S(1)} %get-tuple-element.65), channel_id=1, source_target_pairs={{0,2},{1,3},{2,0},{3,1},{4,6},{5,7},{6,4},{7,5},{8,10},{9,11},{10,... | collective-permute-start | bytes 393224 | tf_op jit(solution)/shard_map/ppermute | solution.py:361
  122.2 1.4 %collective-permute-start.16 = (f32[16,2048]{1,0:T(8,128)S(1)}, f32[16,2048]{1,0:T(8,128)S(1)}, u32[]{:S(2)}, u32[]{:S(2)}) collective-permute-start(f32[16,2048]{1,0:T(8,128)S(1)} %get-tuple-element.66), channel_id=1, source_target_pairs={{0,3},{1,0},{2,1},{3,2},{4,7},{5,4},{6,5},{7,6},{8,11},{9,8},{10,9... | collective-permute-start | bytes 393224 | tf_op jit(solution)/shard_map/ppermute | solution.py:361
  123.6 3.4 %collective-permute-done.14.p1 = f32[16,2048]{1,0:T(8,128)S(1)} collective-permute-done((f32[16,2048]{1,0:T(8,128)S(1)}, f32[16,2048]{1,0:T(8,128)S(1)}, u32[]{:S(2)}, u32[]{:S(2)}) %collective-permute-start.14) | collective-permute-done | bytes 131104 | tf_op jit(solution)/shard_map/ppermute | solution.py:361
  127.0 1.4 %collective-permute-done.15.p2 = f32[16,2048]{1,0:T(8,128)S(1)} collective-permute-done((f32[16,2048]{1,0:T(8,128)S(1)}, f32[16,2048]{1,0:T(8,128)S(1)}, u32[]{:S(2)}, u32[]{:S(2)}) %collective-permute-start.15) | collective-permute-done | bytes 131104 | tf_op jit(solution)/shard_map/ppermute | solution.py:361
  (28 shorter events, 6.0 us)
Async XLA Ops:
  0.0 24.9 %copy-start.2 = (f32[128,64]{0,1:T(8,128)S(1)}, f32[128,64]{0,1:T(8,128)}, u32[]{:S(2)}) copy-start(f32[128,64]{0,1:T(8,128)} %param.4) | copy-start | bytes 98308
  1.2 9.0 %collective-permute-start = (f32[128,512]{1,0:T(8,128)S(1)}, f32[128,512]{1,0:T(8,128)S(1)}, u32[]{:S(2)}, u32[]{:S(2)}) collective-permute-start(f32[128,512]{1,0:T(8,128)S(1)} %get-tuple-element.78), channel_id=1, source_target_pairs={{0,1},{1,2},{2,3},{3,0},{4,5},{5,6},{6,7},{7,4},{8,9},{9,10},{10,1... | collective-permute-start | bytes 786440 | tf_op jit(solution)/shard_map/ppermute | solution.py:339
  3.4 14.0 %collective-permute-start.1 = (f32[128,512]{1,0:T(8,128)S(1)}, f32[128,512]{1,0:T(8,128)S(1)}, u32[]{:S(2)}, u32[]{:S(2)}) collective-permute-start(f32[128,512]{1,0:T(8,128)S(1)} %get-tuple-element.77), channel_id=1, source_target_pairs={{0,2},{1,3},{2,0},{3,1},{4,6},{5,7},{6,4},{7,5},{8,10},{9,11},{10,... | collective-permute-start | bytes 786440 | tf_op jit(solution)/shard_map/ppermute | solution.py:339
  6.0 12.4 %collective-permute-start.2 = (f32[128,512]{1,0:T(8,128)S(1)}, f32[128,512]{1,0:T(8,128)S(1)}, u32[]{:S(2)}, u32[]{:S(2)}) collective-permute-start(f32[128,512]{1,0:T(8,128)S(1)} %get-tuple-element.76), channel_id=1, source_target_pairs={{0,3},{1,0},{2,1},{3,2},{4,7},{5,4},{6,5},{7,6},{8,11},{9,8},{10,9... | collective-permute-start | bytes 786440 | tf_op jit(solution)/shard_map/ppermute | solution.py:339
  8.9 15.3 %collective-permute-start.3 = (f32[128,512]{1,0:T(8,128)}, f32[128,512]{1,0:T(8,128)S(1)}, u32[]{:S(2)}, u32[]{:S(2)}) collective-permute-start(f32[128,512]{1,0:T(8,128)} %get-tuple-element.75), channel_id=1, source_target_pairs={{0,1},{1,2},{2,3},{3,0},{4,5},{5,6},{6,7},{7,4},{8,9},{9,10},{10,1... | collective-permute-start | bytes 786440 | tf_op jit(solution)/shard_map/ppermute | solution.py:339
  9.3 21.0 %collective-permute-start.4 = (f32[128,512]{1,0:T(8,128)S(1)}, f32[128,512]{1,0:T(8,128)S(1)}, u32[]{:S(2)}, u32[]{:S(2)}) collective-permute-start(f32[128,512]{1,0:T(8,128)S(1)} %get-tuple-element.74), channel_id=1, source_target_pairs={{0,2},{1,3},{2,0},{3,1},{4,6},{5,7},{6,4},{7,5},{8,10},{9,11},{10,... | collective-permute-start | bytes 786440 | tf_op jit(solution)/shard_map/ppermute | solution.py:339
  10.1 20.2 %collective-permute-start.5 = (f32[128,512]{1,0:T(8,128)S(1)}, f32[128,512]{1,0:T(8,128)S(1)}, u32[]{:S(2)}, u32[]{:S(2)}) collective-permute-start(f32[128,512]{1,0:T(8,128)S(1)} %get-tuple-element.73), channel_id=1, source_target_pairs={{0,3},{1,0},{2,1},{3,2},{4,7},{5,4},{6,5},{7,6},{8,11},{9,8},{10,9... | collective-permute-start | bytes 786440 | tf_op jit(solution)/shard_map/ppermute | solution.py:339
  20.4 15.6 %collective-permute-start.10 = (f32[128,640]{1,0:T(8,128)S(1)}, f32[128,640]{1,0:T(8,128)S(1)}, u32[]{:S(2)}, u32[]{:S(2)}) collective-permute-start(f32[128,640]{1,0:T(8,128)S(1)} %get-tuple-element.68), channel_id=1, source_target_pairs={{0,2},{1,3},{2,0},{3,1},{4,6},{5,7},{6,4},{7,5},{8,10},{9,11},{10,... | collective-permute-start | bytes 983048 | tf_op jit(solution)/shard_map/ppermute | solution.py:339
  21.3 22.4 %collective-permute-start.11 = (f32[128,640]{1,0:T(8,128)}, f32[128,640]{1,0:T(8,128)S(1)}, u32[]{:S(2)}, u32[]{:S(2)}) collective-permute-start(f32[128,640]{1,0:T(8,128)} %get-tuple-element.67), channel_id=1, source_target_pairs={{0,3},{1,0},{2,1},{3,2},{4,7},{5,4},{6,5},{7,6},{8,11},{9,8},{10,9... | collective-permute-start | bytes 983048 | tf_op jit(solution)/shard_map/ppermute | solution.py:339
  24.3 19.5 %collective-permute-start.9 = (f32[128,640]{1,0:T(8,128)S(1)}, f32[128,640]{1,0:T(8,128)S(1)}, u32[]{:S(2)}, u32[]{:S(2)}) collective-permute-start(f32[128,640]{1,0:T(8,128)S(1)} %get-tuple-element.69), channel_id=1, source_target_pairs={{0,1},{1,2},{2,3},{3,0},{4,5},{5,6},{6,7},{7,4},{8,9},{9,10},{10,1... | collective-permute-start | bytes 983048 | tf_op jit(solution)/shard_map/ppermute | solution.py:339
  28.8 0.8 copy-start
  29.6 0.8 copy-start.1
  31.5 17.4 %collective-permute-start.6 = (f32[128,384]{1,0:T(8,128)S(1)}, f32[128,384]{1,0:T(8,128)S(1)}, u32[]{:S(2)}, u32[]{:S(2)}) collective-permute-start(f32[128,384]{1,0:T(8,128)S(1)} %get-tuple-element.72), channel_id=1, source_target_pairs={{0,1},{1,2},{2,3},{3,0},{4,5},{5,6},{6,7},{7,4},{8,9},{9,10},{10,1... | collective-permute-start | bytes 589832 | tf_op jit(solution)/shard_map/ppermute | solution.py:339
  33.1 18.0 %collective-permute-start.7 = (f32[128,384]{1,0:T(8,128)S(1)}, f32[128,384]{1,0:T(8,128)S(1)}, u32[]{:S(2)}, u32[]{:S(2)}) collective-permute-start(f32[128,384]{1,0:T(8,128)S(1)} %get-tuple-element.71), channel_id=1, source_target_pairs={{0,2},{1,3},{2,0},{3,1},{4,6},{5,7},{6,4},{7,5},{8,10},{9,11},{10,... | collective-permute-start | bytes 589832 | tf_op jit(solution)/shard_map/ppermute | solution.py:339
  35.9 15.2 %collective-permute-start.8 = (f32[128,384]{1,0:T(8,128)S(1)}, f32[128,384]{1,0:T(8,128)S(1)}, u32[]{:S(2)}, u32[]{:S(2)}) collective-permute-start(f32[128,384]{1,0:T(8,128)S(1)} %get-tuple-element.70), channel_id=1, source_target_pairs={{0,3},{1,0},{2,1},{3,2},{4,7},{5,4},{6,5},{7,6},{8,11},{9,8},{10,9... | collective-permute-start | bytes 589832 | tf_op jit(solution)/shard_map/ppermute | solution.py:339
  48.3 54.6 %copy-start.3 = (f32[128,64]{0,1:T(8,128)S(1)}, f32[128,64]{0,1:T(8,128)}, u32[]{:S(2)}) copy-start(f32[128,64]{0,1:T(8,128)} %param.5) | copy-start | bytes 98308
  55.0 2.6 %collective-permute-start.12 = (f32[256,128]{1,0:T(8,128)S(1)}, f32[256,128]{1,0:T(8,128)S(1)}, u32[]{:S(2)}, u32[]{:S(2)}) collective-permute-start(f32[256,128]{1,0:T(8,128)S(1)} %get-tuple-element.54), channel_id=1, source_target_pairs={{0,4},{4,0},{1,5},{5,1},{2,6},{6,2},{3,7},{7,3},{8,12},{12,8},{9,1... | collective-permute-start | bytes 393224 | tf_op jit(solution)/shard_map/ppermute | solution.py:320
  97.5 5.5 %collective-permute-start.13 = (f32[256,128]{1,0:T(8,128)S(1)}, f32[256,128]{1,0:T(8,128)S(1)}, u32[]{:S(2)}, u32[]{:S(2)}) collective-permute-start(f32[256,128]{1,0:T(8,128)S(1)} %bitcast.4), channel_id=1, source_target_pairs={{0,4},{4,0},{1,5},{5,1},{2,6},{6,2},{3,7},{7,3},{8,12},{12,8},{9,1... | collective-permute-start | bytes 393224 | tf_op jit(solution)/shard_map/ppermute | solution.py:324
  120.2 6.7 %collective-permute-start.14 = (f32[16,2048]{1,0:T(8,128)S(1)}, f32[16,2048]{1,0:T(8,128)S(1)}, u32[]{:S(2)}, u32[]{:S(2)}) collective-permute-start(f32[16,2048]{1,0:T(8,128)S(1)} %get-tuple-element.64), channel_id=1, source_target_pairs={{0,1},{1,2},{2,3},{3,0},{4,5},{5,6},{6,7},{7,4},{8,9},{9,10},{10,1... | collective-permute-start | bytes 393224 | tf_op jit(solution)/shard_map/ppermute | solution.py:361
  120.5 7.9 %collective-permute-start.15 = (f32[16,2048]{1,0:T(8,128)S(1)}, f32[16,2048]{1,0:T(8,128)S(1)}, u32[]{:S(2)}, u32[]{:S(2)}) collective-permute-start(f32[16,2048]{1,0:T(8,128)S(1)} %get-tuple-element.65), channel_id=1, source_target_pairs={{0,2},{1,3},{2,0},{3,1},{4,6},{5,7},{6,4},{7,5},{8,10},{9,11},{10,... | collective-permute-start | bytes 393224 | tf_op jit(solution)/shard_map/ppermute | solution.py:361
  122.2 7.1 %collective-permute-start.16 = (f32[16,2048]{1,0:T(8,128)S(1)}, f32[16,2048]{1,0:T(8,128)S(1)}, u32[]{:S(2)}, u32[]{:S(2)}) collective-permute-start(f32[16,2048]{1,0:T(8,128)S(1)} %get-tuple-element.66), channel_id=1, source_target_pairs={{0,3},{1,0},{2,1},{3,2},{4,7},{5,4},{6,5},{7,6},{8,11},{9,8},{10,9... | collective-permute-start | bytes 393224 | tf_op jit(solution)/shard_map/ppermute | solution.py:361

commit v4 on v3

--- a/solution.py
+++ b/solution.py
@@ -14,7 +14,7 @@
 in_space = pltpu.with_memory_space_constraint
 SPACE = ("z", "x", "core")
 PARAMS = pltpu.CompilerParams(vmem_limit_bytes=12 * 2**20)
-CHUNKS = (512, 512, 640, 384)
+CHUNKS = (512, 512, 768, 256)
 PLAN = (((16, True), (16, True)), ((8, False), (16, False)), ((16, False), (16, False)))
 
 
@@ -153,8 +153,9 @@
 def gram_kernel(base, first, last, sketch_ref, archive_ref, p1, p2, p3, *refs):
     sofar, refs = refs[: not first], refs[not first :]
     sums, refs = refs[: 1 + last], refs[1 + last :]
-    (high_ref, low_ref), refs = refs[:2], refs[2:]
-    sketch_out, (held, red, sem, *turned) = refs[:first], refs[first:]
+    halves_out, refs = refs[:2], refs[2:]
+    sketch_out, (held, red, sem, *extra) = refs[:first], refs[first:]
+    high_ref, low_ref = extra[:2] if first else halves_out
     t = lax.axis_index("tm")
     step = held.shape[2]
     sources = (own_cells(archive_ref, t, base, step), p1, p2, p3)
@@ -163,8 +164,8 @@
         copy.start()
     if first:
         k = sketch_ref.shape[1]
-        turned[0][...] = sketch_ref[...].T
-        wl = jnp.concatenate([turned[0][pl.ds(j, k // 4, stride=4), :] for j in range(4)], 0)
+        extra[2][...] = sketch_ref[...].T
+        wl = jnp.concatenate([extra[2][pl.ds(j, k // 4, stride=4), :] for j in range(4)], 0)
         sketch_out[0][...] = wl
     else:
         wl = sketch_ref[...]
@@ -172,6 +173,9 @@
     for d, copy in enumerate(copies):
         copy.wait()
         store_halves(t, d, held.at[d], high_ref, low_ref)
+    outward = [pltpu.make_async_copy(a, b, sem.at[4 + i]) for i, (a, b) in enumerate(zip(extra[:2], halves_out))]
+    for copy in outward:
+        copy.start()
     halves = [(ref[: 2 * k, :], ref[2 * k :, :]) for ref in (high_ref, low_ref)]
 
     def block(i, j):
@@ -180,17 +184,20 @@
 
     blank = jnp.zeros_like(wl)
     wide = jnp.concatenate([jnp.concatenate([wl, blank], 1), jnp.concatenate([blank, wl], 1)], 0)
-    own = [mtm(wide, block(i, j)) for i, j in ((0, 0), (1, 1), (0, 1))]
+    sketched = mm(jnp.concatenate([block(0, 0), block(1, 1), block(0, 1)], 0), wide)
+    near = lax.broadcasted_iota(jnp.int32, (k, 2 * r), 1) < r
 
     def add(at, value):
         to = slice(at * r, at * r + value.shape[0])
         red[to, :] = value if first else sofar[0][to, :] + value
 
-    for w in range(4):
-        add(w, own[w // 2][w % 2 * r : (w % 2 + 1) * r, w % 2 * k : (w % 2 + 1) * k])
-    beside = mm(jnp.concatenate([own[0][:r, k:], own[1][:r, k:]], 0), wl)
-    add(4, jnp.concatenate([beside[:r], beside[r:]], 1))
-    add(5, mm(own[2], wide))
+    beside = []
+    for i in range(2):
+        top, bottom = sketched[2 * i * k : (2 * i + 1) * k], sketched[(2 * i + 1) * k : (2 * i + 2) * k]
+        add(2 * i, jnp.where(near, top, bottom).T)
+        beside.append(top[:, r:])
+    add(4, mtm(wl, jnp.concatenate(beside, 1)))
+    add(5, mtm(wide, sketched[4 * k :]))
     if first:
         red[7 * r :, :] = jnp.zeros((r, k), jnp.float32)
     else:
@@ -202,26 +209,28 @@
         sums[1][...] = red[pl.ds(pl.multiple_of((1 - core) * half, half), half), :]
     else:
         sums[0][...] = red[...]
+    for copy in outward:
+        copy.wait()
 
 
 def grams(base, sketch, archive, parts, sofar, last):
     first = not sofar
     k, r = max(sketch.shape), min(sketch.shape)
     rows, step = parts[0].shape
-    halves = ((jax.ShapeDtypeStruct if first else pltpu.VMEM)((4 * k, step), jnp.bfloat16),) * 2
+    halves = ((pltpu.HBM if first else pltpu.VMEM)((4 * k, step), jnp.bfloat16),) * 2
     sums = (jax.ShapeDtypeStruct((4 * r if last else 8 * r, k), jnp.float32),) * (1 + last)
     ordered = (jax.ShapeDtypeStruct((k, r), jnp.float32),) * first
     return pl.pallas_call(
         functools.partial(gram_kernel, base, first, last),
         out_shape=sums + halves + ordered,
         in_specs=[VMEM] + [ANY] * 4 + [VMEM] * len(sofar),
-        out_specs=(VMEM,) * (len(sums) + 2 + first),
+        out_specs=(VMEM,) * len(sums) + (ANY if first else VMEM,) * 2 + (VMEM,) * first,
         scratch_shapes=[
             pltpu.VMEM((4, rows, step), jnp.float32),
             pltpu.VMEM((8 * r, k), jnp.float32),
-            pltpu.SemaphoreType.DMA((4,)),
+            pltpu.SemaphoreType.DMA((6,)),
         ]
-        + [pltpu.VMEM((k, r), jnp.float32)] * first,
+        + ([pltpu.VMEM((4 * k, step), jnp.bfloat16)] * 2 + [pltpu.VMEM((k, r), jnp.float32)]) * first,
         compiler_params=PARAMS,
         cost_estimate=pl.CostEstimate(flops=128 * k * k * step, bytes_accessed=48 * k * step, transcendentals=0),
         name="grams",
@@ -248,7 +257,8 @@
     at = 0
     for high, low in zip((early.at[0], *highs[1:]), (early.at[1], *lows[1:])):
         step = high.shape[1]
-        total[:, at : at + step] = dot(a, high[...]) + (dot(a, low[...]) + dot(b, high[...]))
+        both = dot(jnp.concatenate([a, b], 0), high[...])
+        total[:, at : at + step] = both[: a.shape[0]] + (both[a.shape[0] :] + dot(a, low[...]))
         at += step
     per = outs[0].shape[0]
     for d, out in enumerate(outs):
@@ -316,11 +326,12 @@
 
 def sum_everywhere(mine, theirs):
     rows, lanes = mine.shape
-    n = lax.axis_size("z")
+    outer, inner = ("x", "tm"), "z"
+    n = lax.axis_size(outer)
     v = mine + lax.ppermute(theirs, "core", ring("core", 1))
-    v = a2a(v.reshape(n, rows // n, lanes), "z").sum(0)
-    v = spread_over(v, ("x", "tm")).sum(0)
-    v = spread_over(v, "z").reshape(rows, lanes)
+    v = a2a(v.reshape(n, rows // n, lanes), outer).sum(0)
+    v = spread_over(v, inner).sum(0)
+    v = spread_over(v, outer).reshape(rows, lanes)
     return v, lax.ppermute(v, "core", ring("core", 1))
 
 
@@ -358,7 +369,7 @@
         low.append(l)
     *sums, h, l = grams(bases[last], sketch, archive, moved[last], sums, True)
     out = modes(*sum_everywhere(*sums), sketch, merge.T, [*high, h], [*low, l])
-    back = {d: lax.ppermute(out[d], "tm", ring("tm", d)) for d in sends}
+    back = {d: lax.ppermute(out[d], "tm", ring("tm", d)) for d in (1, 3, 2)}
     return place([out[0], *(back[d] for d in (1, 2, 3))])
 
 

time: 131 us -> 128 us (0.977)
  blocking collectives: 39.7 us -> 37.6 us
  Pallas kernels: 34.4 us -> 32.8 us
  local copies, waits for them, and re-layouts: 7.81 us -> 6.47 us
    all_to_all x3, blocking collectives: 39.7 us -> 37.6 us  [a2a(): return lax.all_to_all(v, axis, 0, 0, tiled=True)]
    unnamed x8 -> x4, local copies, waits for them, and re-layouts: 1.61 us -> 0.01 us
  transfers between devices with their start and end apart: 17 -> 17, of which waited for: 10 -> 10; matrix products, arithmetic and copies ran while one was open for 4% -> 4% of each run, Pallas kernels for 10% -> 9%
where the time goes in v4:
time: 128 us
  blocking collectives  37.6 us (29%)
  Pallas kernels  32.8 us (26%)
  starting transfers between devices  28.6 us (22%)
  waiting for transfers between devices  21.8 us (17%)
  local copies, waits for them, and re-layouts  6.47 us (5%)
    all_to_all x3, blocking collectives, a2a(): return lax.all_to_all(v, axis, 0, 0, tiled=True)  37.6 us
    ppermute x12, starting transfers between devices, send(): lax.ppermute(p, 'tm', ring('tm', d))  18.6 us
    pallas_call x1, Pallas kernels, modes(): pl.pallas_call(functools.partial(modes_kernel, count), out_shape=(jax.Sha...  16.9 us
    pallas_call x4, Pallas kernels, grams(): pl.pallas_call(functools.partial(gram_kernel, base, first, last), out_sha...  15.1 us
    ppermute x12, waiting for transfers between devices, send(): lax.ppermute(p, 'tm', ring('tm', d))  14.2 us
    dynamic_slice x4, local copies, waits for them, and re-layouts, send(): pieces = [lax.dynamic_slice_in_dim(source, a, CHUNKS[c], 1) for a in at]  6.44 us
    ppermute x3, waiting for transfers between devices, on_device(): back = {d: lax.ppermute(out[d], 'tm', ring('tm', d)) for d in (1, 3, 2)}  5.69 us
    ppermute x1, starting transfers between devices, sum_everywhere(): return (v, lax.ppermute(v, 'core', ring('core', 1)))  4.26 us
  transfers between devices with their start and end apart: 17, of which 10 were waited for; matrix products, arithmetic and copies ran while one was open for 4% of the time, Pallas kernels for 9%

profile of v4, /device:TPU:1, one launch (start us, length us, event | category | flops | bytes accessed | tf_op | source)
XLA Modules:
  0.0 127.7 jit_solution(8929958449175138684)
XLA Ops:
  0.0 1.2 constant_dynamic-slice_fusion.9
  1.2 2.2 %collective-permute-start = (f32[128,512]{1,0:T(8,128)S(1)}, f32[128,512]{1,0:T(8,128)S(1)}, u32[]{:S(2)}, u32[]{:S(2)}) collective-permute-start(f32[128,512]{1,0:T(8,128)S(1)} %get-tuple-element.78), channel_id=1, source_target_pairs={{0,1},{1,2},{2,3},{3,0},{4,5},{5,6},{6,7},{7,4},{8,9},{9,10},{10,1... | collective-permute-start | bytes 786440 | tf_op jit(solution)/shard_map/ppermute | solution.py:350
  3.4 2.6 %collective-permute-start.1 = (f32[128,512]{1,0:T(8,128)S(1)}, f32[128,512]{1,0:T(8,128)S(1)}, u32[]{:S(2)}, u32[]{:S(2)}) collective-permute-start(f32[128,512]{1,0:T(8,128)S(1)} %get-tuple-element.77), channel_id=1, source_target_pairs={{0,2},{1,3},{2,0},{3,1},{4,6},{5,7},{6,4},{7,5},{8,10},{9,11},{10,... | collective-permute-start | bytes 786440 | tf_op jit(solution)/shard_map/ppermute | solution.py:350
  6.0 1.1 collective-permute-start.2
  7.1 1.9 %constant_dynamic-slice_fusion.6 = (f32[128,512]{1,0:T(8,128)S(1)}, f32[128,512]{1,0:T(8,128)S(1)}, f32[128,512]{1,0:T(8,128)}) fusion(f32[128,8192]{1,0:T(8,128)} %archive_ref.7, s32[]{:T(128)S(6)} %select_n.77, s32[]{:T(128)S(6)} %select_n.76, s32[]{:T(128)S(6)} %select_n.75), kind=kLoop, calls=%fused_computation.6 | loop fusion | bytes 1572876 | tf_op jit(solution)/shard_map/dynamic_slice | solution.py:349
  10.1 1.9 %collective-permute-start.5 = (f32[128,512]{1,0:T(8,128)S(1)}, f32[128,512]{1,0:T(8,128)S(1)}, u32[]{:S(2)}, u32[]{:S(2)}) collective-permute-start(f32[128,512]{1,0:T(8,128)S(1)} %get-tuple-element.73), channel_id=1, source_target_pairs={{0,3},{1,0},{2,1},{3,2},{4,7},{5,4},{6,5},{7,6},{8,11},{9,8},{10,9... | collective-permute-start | bytes 786440 | tf_op jit(solution)/shard_map/ppermute | solution.py:350
  12.0 5.4 %collective-permute-done.1.p2 = f32[128,512]{1,0:T(8,128)S(1)} collective-permute-done((f32[128,512]{1,0:T(8,128)S(1)}, f32[128,512]{1,0:T(8,128)S(1)}, u32[]{:S(2)}, u32[]{:S(2)}) %collective-permute-start.1) | collective-permute-done | bytes 262176 | tf_op jit(solution)/shard_map/ppermute | solution.py:350
  17.4 1.0 collective-permute-done.2.p3
  18.4 2.3 %constant_dynamic-slice_fusion = (f32[128,768]{1,0:T(8,128)}, f32[128,768]{1,0:T(8,128)}, f32[128,768]{1,0:T(8,128)}) fusion(f32[128,8192]{1,0:T(8,128)} %archive_ref.7, s32[]{:T(128)S(6)} %select_n.83, s32[]{:T(128)S(6)} %select_n.82, s32[]{:T(128)S(6)} %select_n.81), kind=kLoop, calls=%fused_computation | loop fusion | bytes 2359308 | tf_op jit(solution)/shard_map/dynamic_slice | solution.py:349
  20.7 1.0 collective-permute-start.10
  21.7 2.9 %collective-permute-start.11 = (f32[128,768]{1,0:T(8,128)}, f32[128,768]{1,0:T(8,128)S(1)}, u32[]{:S(2)}, u32[]{:S(2)}) collective-permute-start(f32[128,768]{1,0:T(8,128)} %get-tuple-element.67), channel_id=1, source_target_pairs={{0,3},{1,0},{2,1},{3,2},{4,7},{5,4},{6,5},{7,6},{8,11},{9,8},{10,9... | collective-permute-start | bytes 1179656 | tf_op jit(solution)/shard_map/ppermute | solution.py:350
  25.2 3.7 %grams.4 = (f32[512,128]{1,0:T(8,128)S(1)}, bf16[512,512]{1,0:T(8,128)(2,1)}, bf16[512,512]{1,0:T(8,128)(2,1)}, f32[128,64]{1,0:T(8,128)S(1)}) custom-call(f32[64,128]{1,0:T(8,128)S(1)} %bitcast.6, f32[128,8192]{1,0:T(8,128)} %archive_ref.7, f32[128,512]{1,0:T(8,128)S(1)} %collective-permute-done.p1, f32[128,512]{1,0:T(8,128)S(1)} %collective-permute-done.1.p2, ...), custom_call_target="tpu_custom_call" | custom-call | flops 1073741824 | bytes 3145728 | tf_op jit(solution)/shard_map/grams/pallas_call | solution.py:223
  29.0 3.7 %grams.5 = (f32[512,128]{1,0:T(8,128)S(1)}, bf16[512,512]{1,0:T(8,128)(2,1)S(1)}, bf16[512,512]{1,0:T(8,128)(2,1)S(1)}) custom-call(f32[128,64]{1,0:T(8,128)S(1)} %get-tuple-element.41.sketch_ref.leaf_ref, f32[128,8192]{1,0:T(8,128)} %archive_ref.7, f32[128,512]{1,0:T(8,128)S(1)} %collective-permute-done.3.p1, f32[128,512]{1,0:T(8,128)S(1)} %collective-permute-done.4.p2, ...), custom_call_target="tpu_custom_call" | custom-call | flops 1073741824 | bytes 3145728 | tf_op jit(solution)/shard_map/grams/pallas_call | solution.py:223
  32.7 1.1 constant_dynamic-slice_fusion.3
  33.8 1.4 %collective-permute-start.6 = (f32[128,256]{1,0:T(8,128)S(1)}, f32[128,256]{1,0:T(8,128)S(1)}, u32[]{:S(2)}, u32[]{:S(2)}) collective-permute-start(f32[128,256]{1,0:T(8,128)S(1)} %get-tuple-element.72), channel_id=1, source_target_pairs={{0,1},{1,2},{2,3},{3,0},{4,5},{5,6},{6,7},{7,4},{8,9},{9,10},{10,1... | collective-permute-start | bytes 393224 | tf_op jit(solution)/shard_map/ppermute | solution.py:350
  35.2 3.7 %collective-permute-start.7 = (f32[128,256]{1,0:T(8,128)S(1)}, f32[128,256]{1,0:T(8,128)S(1)}, u32[]{:S(2)}, u32[]{:S(2)}) collective-permute-start(f32[128,256]{1,0:T(8,128)S(1)} %get-tuple-element.71), channel_id=1, source_target_pairs={{0,2},{1,3},{2,0},{3,1},{4,6},{5,7},{6,4},{7,5},{8,10},{9,11},{10,... | collective-permute-start | bytes 393224 | tf_op jit(solution)/shard_map/ppermute | solution.py:350
  39.0 6.9 %collective-permute-done.11.p3 = f32[128,768]{1,0:T(8,128)S(1)} collective-permute-done((f32[128,768]{1,0:T(8,128)}, f32[128,768]{1,0:T(8,128)S(1)}, u32[]{:S(2)}, u32[]{:S(2)}) %collective-permute-start.11) | collective-permute-done | bytes 393248 | tf_op jit(solution)/shard_map/ppermute | solution.py:350
  46.6 4.6 %grams.6 = (f32[512,128]{1,0:T(8,128)S(1)}, bf16[512,768]{1,0:T(8,128)(2,1)S(1)}, bf16[512,768]{1,0:T(8,128)(2,1)S(1)}) custom-call(f32[128,64]{1,0:T(8,128)S(1)} %get-tuple-element.41.sketch_ref.leaf_ref, f32[128,8192]{1,0:T(8,128)} %archive_ref.7, f32[128,768]{1,0:T(8,128)} %collective-permute-done.9.p1, f32[128,768]{1,0:T(8,128)S(1)} %collective-permute-done.10.p2, ...), custom_call_target="tpu_custom_call" | custom-call | flops 1610612736 | bytes 4718592 | tf_op jit(solution)/shard_map/grams/pallas_call | solution.py:223
  51.3 3.1 %grams.7 = (f32[256,128]{1,0:T(8,128)S(1)}, f32[256,128]{1,0:T(8,128)S(1)}, bf16[512,256]{1,0:T(8,128)(2,1)S(1)}, bf16[512,256]{1,0:T(8,128)(2,1)S(1)}) custom-call(f32[128,64]{1,0:T(8,128)S(1)} %get-tuple-element.41.sketch_ref.leaf_ref, f32[128,8192]{1,0:T(8,128)} %archive_ref.7, f32[128,256]{1,0:T(8,128)S(1)} %collective-permute-done.6.p1, ...), custom_call_target="tpu_custom_call" | custom-call | flops 536870912 | bytes 1572864 | tf_op jit(solution)/shard_map/grams/pallas_call | solution.py:223
  54.4 2.4 %collective-permute-start.12 = (f32[256,128]{1,0:T(8,128)S(1)}, f32[256,128]{1,0:T(8,128)S(1)}, u32[]{:S(2)}, u32[]{:S(2)}) collective-permute-start(f32[256,128]{1,0:T(8,128)S(1)} %get-tuple-element.54), channel_id=1, source_target_pairs={{0,4},{4,0},{1,5},{5,1},{2,6},{6,2},{3,7},{7,3},{8,12},{12,8},{9,1... | collective-permute-start | bytes 393224 | tf_op jit(solution)/shard_map/ppermute | solution.py:331
  56.8 1.0 collective-permute-done.12
  57.8 12.2 %all_to_all.15 = f32[16,16,128]{2,1,0:T(8,128)S(1)} all-to-all(f32[16,16,128]{2,1,0:T(8,128)S(1)} %bitcast.8), channel_id=1, replica_groups=mesh['z'=8,'x'=4,'core'=2,'tm'=4] {'x','tm'}, dimensions={0} | all-to-all | bytes 262144 | tf_op jit(solution)/shard_map/all_to_all | solution.py:319
  70.0 15.2 %all_to_all.16 = f32[8,16,128]{2,1,0:T(8,128)S(1)} all-to-all(f32[8,16,128]{2,1,0:T(8,128)S(1)} %broadcast_in_dim.4), channel_id=1, replica_groups=mesh['z'=8,'x'=4,'core'=2,'tm'=4] {'z'}, dimensions={0} | all-to-all | bytes 131072 | tf_op jit(solution)/shard_map/all_to_all | solution.py:319
  85.2 10.2 %all_to_all.17 = f32[16,16,128]{2,1,0:T(8,128)S(1)} all-to-all(f32[16,16,128]{2,1,0:T(8,128)S(1)} %broadcast_in_dim.5), channel_id=1, replica_groups=mesh['z'=8,'x'=4,'core'=2,'tm'=4] {'x','tm'}, dimensions={0} | all-to-all | bytes 262144 | tf_op jit(solution)/shard_map/all_to_all | solution.py:319
  95.4 4.3 %collective-permute-start.13 = (f32[256,128]{1,0:T(8,128)S(1)}, f32[256,128]{1,0:T(8,128)S(1)}, u32[]{:S(2)}, u32[]{:S(2)}) collective-permute-start(f32[256,128]{1,0:T(8,128)S(1)} %bitcast.4), channel_id=1, source_target_pairs={{0,4},{4,0},{1,5},{5,1},{2,6},{6,2},{3,7},{7,3},{8,12},{12,8},{9,1... | collective-permute-start | bytes 393224 | tf_op jit(solution)/shard_map/ppermute | solution.py:335
  99.7 1.0 collective-permute-done.13.other_ref
  100.7 16.9 %modes.1 = (f32[16,2048]{1,0:T(8,128)S(1)}, f32[16,2048]{1,0:T(8,128)S(1)}, f32[16,2048]{1,0:T(8,128)S(1)}, f32[16,2048]{1,0:T(8,128)S(1)}) custom-call(f32[256,128]{1,0:T(8,128)S(1)} %bitcast.5, f32[256,128]{1,0:T(8,128)S(1)} %collective-permute-done.13.other_ref, f32[128,64]{1,0:T(8,128)S(1)} %get-tuple-element.41.sketch_ref.leaf_ref, ...), custom_call_target="tpu_custom_call" | custom-call | tf_op jit(solution)/shard_map/modes/pallas_call | solution.py:271
  117.9 2.0 %collective-permute-start.15 = (f32[16,2048]{1,0:T(8,128)S(1)}, f32[16,2048]{1,0:T(8,128)S(1)}, u32[]{:S(2)}, u32[]{:S(2)}) collective-permute-start(f32[16,2048]{1,0:T(8,128)S(1)} %get-tuple-element.65), channel_id=1, source_target_pairs={{0,2},{1,3},{2,0},{3,1},{4,6},{5,7},{6,4},{7,5},{8,10},{9,11},{10,... | collective-permute-start | bytes 393224 | tf_op jit(solution)/shard_map/ppermute | solution.py:372
  119.8 1.1 collective-permute-start.16
  121.0 3.1 %collective-permute-done.14.p1 = f32[16,2048]{1,0:T(8,128)S(1)} collective-permute-done((f32[16,2048]{1,0:T(8,128)S(1)}, f32[16,2048]{1,0:T(8,128)S(1)}, u32[]{:S(2)}, u32[]{:S(2)}) %collective-permute-start.14) | collective-permute-done | bytes 131104 | tf_op jit(solution)/shard_map/ppermute | solution.py:372
  124.1 1.8 %collective-permute-done.15.p2 = f32[16,2048]{1,0:T(8,128)S(1)} collective-permute-done((f32[16,2048]{1,0:T(8,128)S(1)}, f32[16,2048]{1,0:T(8,128)S(1)}, u32[]{:S(2)}, u32[]{:S(2)}) %collective-permute-start.15) | collective-permute-done | bytes 131104 | tf_op jit(solution)/shard_map/ppermute | solution.py:372
  126.7 0.8 place.1
  (24 shorter events, 3.8 us)
Async XLA Ops:
  0.0 25.2 %copy-start = (f32[128,64]{0,1:T(8,128)S(1)}, f32[128,64]{0,1:T(8,128)}, u32[]{:S(2)}) copy-start(f32[128,64]{0,1:T(8,128)} %param.4) | copy-start | bytes 98308
  1.2 9.0 %collective-permute-start = (f32[128,512]{1,0:T(8,128)S(1)}, f32[128,512]{1,0:T(8,128)S(1)}, u32[]{:S(2)}, u32[]{:S(2)}) collective-permute-start(f32[128,512]{1,0:T(8,128)S(1)} %get-tuple-element.78), channel_id=1, source_target_pairs={{0,1},{1,2},{2,3},{3,0},{4,5},{5,6},{6,7},{7,4},{8,9},{9,10},{10,1... | collective-permute-start | bytes 786440 | tf_op jit(solution)/shard_map/ppermute | solution.py:350
  3.4 14.0 %collective-permute-start.1 = (f32[128,512]{1,0:T(8,128)S(1)}, f32[128,512]{1,0:T(8,128)S(1)}, u32[]{:S(2)}, u32[]{:S(2)}) collective-permute-start(f32[128,512]{1,0:T(8,128)S(1)} %get-tuple-element.77), channel_id=1, source_target_pairs={{0,2},{1,3},{2,0},{3,1},{4,6},{5,7},{6,4},{7,5},{8,10},{9,11},{10,... | collective-permute-start | bytes 786440 | tf_op jit(solution)/shard_map/ppermute | solution.py:350
  6.0 12.4 %collective-permute-start.2 = (f32[128,512]{1,0:T(8,128)S(1)}, f32[128,512]{1,0:T(8,128)S(1)}, u32[]{:S(2)}, u32[]{:S(2)}) collective-permute-start(f32[128,512]{1,0:T(8,128)S(1)} %get-tuple-element.76), channel_id=1, source_target_pairs={{0,3},{1,0},{2,1},{3,2},{4,7},{5,4},{6,5},{7,6},{8,11},{9,8},{10,9... | collective-permute-start | bytes 786440 | tf_op jit(solution)/shard_map/ppermute | solution.py:350
  8.9 15.7 %collective-permute-start.3 = (f32[128,512]{1,0:T(8,128)}, f32[128,512]{1,0:T(8,128)S(1)}, u32[]{:S(2)}, u32[]{:S(2)}) collective-permute-start(f32[128,512]{1,0:T(8,128)} %get-tuple-element.75), channel_id=1, source_target_pairs={{0,1},{1,2},{2,3},{3,0},{4,5},{5,6},{6,7},{7,4},{8,9},{9,10},{10,1... | collective-permute-start | bytes 786440 | tf_op jit(solution)/shard_map/ppermute | solution.py:350
  9.3 19.6 %collective-permute-start.4 = (f32[128,512]{1,0:T(8,128)S(1)}, f32[128,512]{1,0:T(8,128)S(1)}, u32[]{:S(2)}, u32[]{:S(2)}) collective-permute-start(f32[128,512]{1,0:T(8,128)S(1)} %get-tuple-element.74), channel_id=1, source_target_pairs={{0,2},{1,3},{2,0},{3,1},{4,6},{5,7},{6,4},{7,5},{8,10},{9,11},{10,... | collective-permute-start | bytes 786440 | tf_op jit(solution)/shard_map/ppermute | solution.py:350
  10.1 18.9 %collective-permute-start.5 = (f32[128,512]{1,0:T(8,128)S(1)}, f32[128,512]{1,0:T(8,128)S(1)}, u32[]{:S(2)}, u32[]{:S(2)}) collective-permute-start(f32[128,512]{1,0:T(8,128)S(1)} %get-tuple-element.73), channel_id=1, source_target_pairs={{0,3},{1,0},{2,1},{3,2},{4,7},{5,4},{6,5},{7,6},{8,11},{9,8},{10,9... | collective-permute-start | bytes 786440 | tf_op jit(solution)/shard_map/ppermute | solution.py:350
  20.7 18.3 %collective-permute-start.10 = (f32[128,768]{1,0:T(8,128)}, f32[128,768]{1,0:T(8,128)S(1)}, u32[]{:S(2)}, u32[]{:S(2)}) collective-permute-start(f32[128,768]{1,0:T(8,128)} %get-tuple-element.68), channel_id=1, source_target_pairs={{0,2},{1,3},{2,0},{3,1},{4,6},{5,7},{6,4},{7,5},{8,10},{9,11},{10,... | collective-permute-start | bytes 1179656 | tf_op jit(solution)/shard_map/ppermute | solution.py:350
  21.7 24.2 %collective-permute-start.11 = (f32[128,768]{1,0:T(8,128)}, f32[128,768]{1,0:T(8,128)S(1)}, u32[]{:S(2)}, u32[]{:S(2)}) collective-permute-start(f32[128,768]{1,0:T(8,128)} %get-tuple-element.67), channel_id=1, source_target_pairs={{0,3},{1,0},{2,1},{3,2},{4,7},{5,4},{6,5},{7,6},{8,11},{9,8},{10,9... | collective-permute-start | bytes 1179656 | tf_op jit(solution)/shard_map/ppermute | solution.py:350
  24.6 22.0 %collective-permute-start.9 = (f32[128,768]{1,0:T(8,128)}, f32[128,768]{1,0:T(8,128)}, u32[]{:S(2)}, u32[]{:S(2)}) collective-permute-start(f32[128,768]{1,0:T(8,128)} %get-tuple-element.69), channel_id=1, source_target_pairs={{0,1},{1,2},{2,3},{3,0},{4,5},{5,6},{6,7},{7,4},{8,9},{9,10},{10,1... | collective-permute-start | bytes 1179656 | tf_op jit(solution)/shard_map/ppermute | solution.py:350
  33.8 17.4 %collective-permute-start.6 = (f32[128,256]{1,0:T(8,128)S(1)}, f32[128,256]{1,0:T(8,128)S(1)}, u32[]{:S(2)}, u32[]{:S(2)}) collective-permute-start(f32[128,256]{1,0:T(8,128)S(1)} %get-tuple-element.72), channel_id=1, source_target_pairs={{0,1},{1,2},{2,3},{3,0},{4,5},{5,6},{6,7},{7,4},{8,9},{9,10},{10,1... | collective-permute-start | bytes 393224 | tf_op jit(solution)/shard_map/ppermute | solution.py:350
  35.2 16.0 %collective-permute-start.7 = (f32[128,256]{1,0:T(8,128)S(1)}, f32[128,256]{1,0:T(8,128)S(1)}, u32[]{:S(2)}, u32[]{:S(2)}) collective-permute-start(f32[128,256]{1,0:T(8,128)S(1)} %get-tuple-element.71), channel_id=1, source_target_pairs={{0,2},{1,3},{2,0},{3,1},{4,6},{5,7},{6,4},{7,5},{8,10},{9,11},{10,... | collective-permute-start | bytes 393224 | tf_op jit(solution)/shard_map/ppermute | solution.py:350
  39.0 12.3 %collective-permute-start.8 = (f32[128,256]{1,0:T(8,128)S(1)}, f32[128,256]{1,0:T(8,128)S(1)}, u32[]{:S(2)}, u32[]{:S(2)}) collective-permute-start(f32[128,256]{1,0:T(8,128)S(1)} %get-tuple-element.70), channel_id=1, source_target_pairs={{0,3},{1,0},{2,1},{3,2},{4,7},{5,4},{6,5},{7,6},{8,11},{9,8},{10,9... | collective-permute-start | bytes 393224 | tf_op jit(solution)/shard_map/ppermute | solution.py:350
  51.2 49.4 %copy-start.1 = (f32[128,64]{0,1:T(8,128)S(1)}, f32[128,64]{0,1:T(8,128)}, u32[]{:S(2)}) copy-start(f32[128,64]{0,1:T(8,128)} %param.5) | copy-start | bytes 98308
  54.4 3.4 %collective-permute-start.12 = (f32[256,128]{1,0:T(8,128)S(1)}, f32[256,128]{1,0:T(8,128)S(1)}, u32[]{:S(2)}, u32[]{:S(2)}) collective-permute-start(f32[256,128]{1,0:T(8,128)S(1)} %get-tuple-element.54), channel_id=1, source_target_pairs={{0,4},{4,0},{1,5},{5,1},{2,6},{6,2},{3,7},{7,3},{8,12},{12,8},{9,1... | collective-permute-start | bytes 393224 | tf_op jit(solution)/shard_map/ppermute | solution.py:331
  95.4 5.2 %collective-permute-start.13 = (f32[256,128]{1,0:T(8,128)S(1)}, f32[256,128]{1,0:T(8,128)S(1)}, u32[]{:S(2)}, u32[]{:S(2)}) collective-permute-start(f32[256,128]{1,0:T(8,128)S(1)} %bitcast.4), channel_id=1, source_target_pairs={{0,4},{4,0},{1,5},{5,1},{2,6},{6,2},{3,7},{7,3},{8,12},{12,8},{9,1... | collective-permute-start | bytes 393224 | tf_op jit(solution)/shard_map/ppermute | solution.py:335
  117.6 6.5 %collective-permute-start.14 = (f32[16,2048]{1,0:T(8,128)S(1)}, f32[16,2048]{1,0:T(8,128)S(1)}, u32[]{:S(2)}, u32[]{:S(2)}) collective-permute-start(f32[16,2048]{1,0:T(8,128)S(1)} %get-tuple-element.64), channel_id=1, source_target_pairs={{0,1},{1,2},{2,3},{3,0},{4,5},{5,6},{6,7},{7,4},{8,9},{9,10},{10,1... | collective-permute-start | bytes 393224 | tf_op jit(solution)/shard_map/ppermute | solution.py:372
  117.9 8.1 %collective-permute-start.15 = (f32[16,2048]{1,0:T(8,128)S(1)}, f32[16,2048]{1,0:T(8,128)S(1)}, u32[]{:S(2)}, u32[]{:S(2)}) collective-permute-start(f32[16,2048]{1,0:T(8,128)S(1)} %get-tuple-element.65), channel_id=1, source_target_pairs={{0,2},{1,3},{2,0},{3,1},{4,6},{5,7},{6,4},{7,5},{8,10},{9,11},{10,... | collective-permute-start | bytes 393224 | tf_op jit(solution)/shard_map/ppermute | solution.py:372
  119.8 6.8 %collective-permute-start.16 = (f32[16,2048]{1,0:T(8,128)S(1)}, f32[16,2048]{1,0:T(8,128)S(1)}, u32[]{:S(2)}, u32[]{:S(2)}) collective-permute-start(f32[16,2048]{1,0:T(8,128)S(1)} %get-tuple-element.66), channel_id=1, source_target_pairs={{0,3},{1,0},{2,1},{3,2},{4,7},{5,4},{6,5},{7,6},{8,11},{9,8},{10,9... | collective-permute-start | bytes 393224 | tf_op jit(solution)/shard_map/ppermute | solution.py:372

commit v5 on v4

--- a/solution.py
+++ b/solution.py
@@ -237,16 +237,19 @@
     )(sketch, in_space(archive, pltpu.HBM), *parts, *sofar)
 
 
-def modes_kernel(count, mine_ref, other_ref, leaf_ref, merge_ref, *refs):
+def modes_kernel(count, pieces, sum_ref, leaf_ref, merge_ref, *refs):
     highs, lows, outs, (red, total, early, sem) = refs[:count], refs[count : 2 * count], refs[2 * count : -4], refs[-4:]
     fetches = [pltpu.make_async_copy(s[0], early.at[i], sem.at[i]) for i, s in enumerate((highs, lows))]
     for fetch in fetches:
         fetch.start()
     t = lax.axis_index("tm")
     core = lax.axis_index("core")
-    half = mine_ref.shape[0]
-    red[pl.ds(pl.multiple_of(core * half, half), half), :] = mine_ref[...]
-    red[pl.ds(pl.multiple_of((1 - core) * half, half), half), :] = other_ref[...]
+    half = sum_ref.shape[0] // 2
+    rows = half // pieces
+    for i in range(pieces):
+        for h, side in enumerate((core, 1 - core)):
+            at = pl.multiple_of(side * half + i * rows, rows)
+            red[pl.ds(at, rows), :] = sum_ref[(2 * i + h) * rows : (2 * i + h + 1) * rows, :]
     a, b = split(mm(*combine(red, leaf_ref[...], merge_ref[...])))
 
     def dot(a, b):
@@ -265,13 +268,13 @@
         out[...] = total[pl.ds(pl.multiple_of(lax.rem(t + d, 4) * per, per), per), :]
 
 
-def modes(mine, other, leaf, merge, high, low):
+def modes(total, leaf, merge, high, low):
     k, r = leaf.shape
     count, cells = len(high), sum(h.shape[1] for h in high)
     return pl.pallas_call(
-        functools.partial(modes_kernel, count),
+        functools.partial(modes_kernel, count, lax.axis_size(("x", "tm"))),
         out_shape=(jax.ShapeDtypeStruct((r // 4, cells), jnp.float32),) * 4,
-        in_specs=[VMEM] * 4 + ([ANY] + [VMEM] * (count - 1)) * 2,
+        in_specs=[VMEM] * 3 + ([ANY] + [VMEM] * (count - 1)) * 2,
         out_specs=(VMEM,) * 4,
         scratch_shapes=[
             pltpu.VMEM((8 * r, k), jnp.float32),
@@ -281,7 +284,7 @@
         ],
         compiler_params=PARAMS,
         name="modes",
-    )(mine, other, leaf, merge, *(in_space(v, pltpu.VMEM if i else pltpu.HBM) for s in (high, low) for i, v in enumerate(s)))
+    )(total, leaf, merge, *(in_space(v, pltpu.VMEM if i else pltpu.HBM) for s in (high, low) for i, v in enumerate(s)))
 
 
 def place_kernel(p0, p1, p2, p3, out_ref, sem):
@@ -331,8 +334,8 @@
     v = mine + lax.ppermute(theirs, "core", ring("core", 1))
     v = a2a(v.reshape(n, rows // n, lanes), outer).sum(0)
     v = spread_over(v, inner).sum(0)
-    v = spread_over(v, outer).reshape(rows, lanes)
-    return v, lax.ppermute(v, "core", ring("core", 1))
+    other = lax.ppermute(v, "core", ring("core", 1))
+    return spread_over(jnp.concatenate([v, other], 0), outer).reshape(2 * rows, lanes)
 
 
 def on_device(archive, leaf, merge):
@@ -368,7 +371,7 @@
         high.append(h)
         low.append(l)
     *sums, h, l = grams(bases[last], sketch, archive, moved[last], sums, True)
-    out = modes(*sum_everywhere(*sums), sketch, merge.T, [*high, h], [*low, l])
+    out = modes(sum_everywhere(*sums), sketch, merge.T, [*high, h], [*low, l])
     back = {d: lax.ppermute(out[d], "tm", ring("tm", d)) for d in (1, 3, 2)}
     return place([out[0], *(back[d] for d in (1, 2, 3))])
 

time: 128 us -> 127 us (level)
  waiting for transfers between devices: 21.8 us -> 19.9 us
    ppermute x3, waiting for transfers between devices: 5.69 us -> 3.96 us  [on_device(): back = {d: lax.ppermute(out[d], 'tm', ring('tm', d)) for d in (1, 3, 2)}]
  transfers between devices with their start and end apart: 17 -> 17, of which waited for: 10 -> 9; matrix products, arithmetic and copies ran while one was open for 4% -> 4% of each run, Pallas kernels for 9% -> 10%
where the time goes in v5:
time: 127 us; the launch traced here: 126 us
  blocking collectives  38.1 us (30%)
  Pallas kernels  32.8 us (26%)
  starting transfers between devices  27.8 us (22%)
  waiting for transfers between devices  19.9 us (16%)
  local copies, waits for them, and re-layouts  6.48 us (5%)
    all_to_all x3, blocking collectives, a2a(): return lax.all_to_all(v, axis, 0, 0, tiled=True)  38.1 us
    ppermute x12, starting transfers between devices, send(): lax.ppermute(p, 'tm', ring('tm', d))  18.6 us
    pallas_call x1, Pallas kernels, modes(): pl.pallas_call(functools.partial(modes_kernel, count, lax.axis_size(('x',...  16.9 us
    pallas_call x4, Pallas kernels, grams(): pl.pallas_call(functools.partial(gram_kernel, base, first, last), out_sha...  15.1 us
    ppermute x12, waiting for transfers between devices, send(): lax.ppermute(p, 'tm', ring('tm', d))  14.2 us
    dynamic_slice x4, local copies, waits for them, and re-layouts, send(): pieces = [lax.dynamic_slice_in_dim(source, a, CHUNKS[c], 1) for a in at]  6.44 us
    ppermute x3, waiting for transfers between devices, on_device(): back = {d: lax.ppermute(out[d], 'tm', ring('tm', d)) for d in (1, 3, 2)}  3.96 us
    ppermute x3, starting transfers between devices, on_device(): back = {d: lax.ppermute(out[d], 'tm', ring('tm', d)) for d in (1, 3, 2)}  3.54 us
  transfers between devices with their start and end apart: 17, of which 9 were waited for; matrix products, arithmetic and copies ran while one was open for 4% of the time, Pallas kernels for 10%

profile of v5, /device:TPU:1, one launch (start us, length us, event | category | flops | bytes accessed | tf_op | source)
XLA Modules:
  0.0 125.5 jit_solution(10102730231737745343)
XLA Ops:
  0.0 1.2 constant_dynamic-slice_fusion.9
  1.2 2.2 %collective-permute-start = (f32[128,512]{1,0:T(8,128)S(1)}, f32[128,512]{1,0:T(8,128)S(1)}, u32[]{:S(2)}, u32[]{:S(2)}) collective-permute-start(f32[128,512]{1,0:T(8,128)S(1)} %get-tuple-element.78), channel_id=1, source_target_pairs={{0,1},{1,2},{2,3},{3,0},{4,5},{5,6},{6,7},{7,4},{8,9},{9,10},{10,1... | collective-permute-start | bytes 786440 | tf_op jit(solution)/shard_map/ppermute | solution.py:353
  3.4 2.6 %collective-permute-start.1 = (f32[128,512]{1,0:T(8,128)S(1)}, f32[128,512]{1,0:T(8,128)S(1)}, u32[]{:S(2)}, u32[]{:S(2)}) collective-permute-start(f32[128,512]{1,0:T(8,128)S(1)} %get-tuple-element.77), channel_id=1, source_target_pairs={{0,2},{1,3},{2,0},{3,1},{4,6},{5,7},{6,4},{7,5},{8,10},{9,11},{10,... | collective-permute-start | bytes 786440 | tf_op jit(solution)/shard_map/ppermute | solution.py:353
  6.0 1.1 collective-permute-start.2
  7.1 1.9 %constant_dynamic-slice_fusion.6 = (f32[128,512]{1,0:T(8,128)S(1)}, f32[128,512]{1,0:T(8,128)S(1)}, f32[128,512]{1,0:T(8,128)}) fusion(f32[128,8192]{1,0:T(8,128)} %archive_ref.7, s32[]{:T(128)S(6)} %select_n.77, s32[]{:T(128)S(6)} %select_n.76, s32[]{:T(128)S(6)} %select_n.75), kind=kLoop, calls=%fused_computation.7 | loop fusion | bytes 1572876 | tf_op jit(solution)/shard_map/dynamic_slice | solution.py:352
  9.3 0.8 collective-permute-start.4
  10.1 1.9 %collective-permute-start.5 = (f32[128,512]{1,0:T(8,128)S(1)}, f32[128,512]{1,0:T(8,128)S(1)}, u32[]{:S(2)}, u32[]{:S(2)}) collective-permute-start(f32[128,512]{1,0:T(8,128)S(1)} %get-tuple-element.73), channel_id=1, source_target_pairs={{0,3},{1,0},{2,1},{3,2},{4,7},{5,4},{6,5},{7,6},{8,11},{9,8},{10,9... | collective-permute-start | bytes 786440 | tf_op jit(solution)/shard_map/ppermute | solution.py:353
  12.0 5.4 %collective-permute-done.1.p2 = f32[128,512]{1,0:T(8,128)S(1)} collective-permute-done((f32[128,512]{1,0:T(8,128)S(1)}, f32[128,512]{1,0:T(8,128)S(1)}, u32[]{:S(2)}, u32[]{:S(2)}) %collective-permute-start.1) | collective-permute-done | bytes 262176 | tf_op jit(solution)/shard_map/ppermute | solution.py:353
  17.4 1.0 collective-permute-done.2.p3
  18.4 2.3 %constant_dynamic-slice_fusion = (f32[128,768]{1,0:T(8,128)}, f32[128,768]{1,0:T(8,128)}, f32[128,768]{1,0:T(8,128)}) fusion(f32[128,8192]{1,0:T(8,128)} %archive_ref.7, s32[]{:T(128)S(6)} %select_n.83, s32[]{:T(128)S(6)} %select_n.82, s32[]{:T(128)S(6)} %select_n.81), kind=kLoop, calls=%fused_computation.1 | loop fusion | bytes 2359308 | tf_op jit(solution)/shard_map/dynamic_slice | solution.py:352
  20.7 1.0 collective-permute-start.10
  21.7 2.9 %collective-permute-start.11 = (f32[128,768]{1,0:T(8,128)}, f32[128,768]{1,0:T(8,128)S(1)}, u32[]{:S(2)}, u32[]{:S(2)}) collective-permute-start(f32[128,768]{1,0:T(8,128)} %get-tuple-element.67), channel_id=1, source_target_pairs={{0,3},{1,0},{2,1},{3,2},{4,7},{5,4},{6,5},{7,6},{8,11},{9,8},{10,9... | collective-permute-start | bytes 1179656 | tf_op jit(solution)/shard_map/ppermute | solution.py:353
  25.2 3.7 %grams.4 = (f32[512,128]{1,0:T(8,128)S(1)}, bf16[512,512]{1,0:T(8,128)(2,1)}, bf16[512,512]{1,0:T(8,128)(2,1)}, f32[128,64]{1,0:T(8,128)S(1)}) custom-call(f32[64,128]{1,0:T(8,128)S(1)} %bitcast.5, f32[128,8192]{1,0:T(8,128)} %archive_ref.7, f32[128,512]{1,0:T(8,128)S(1)} %collective-permute-done.p1, f32[128,512]{1,0:T(8,128)S(1)} %collective-permute-done.1.p2, ...), custom_call_target="tpu_custom_call" | custom-call | flops 1073741824 | bytes 3145728 | tf_op jit(solution)/shard_map/grams/pallas_call | solution.py:223
  29.0 3.7 %grams.5 = (f32[512,128]{1,0:T(8,128)S(1)}, bf16[512,512]{1,0:T(8,128)(2,1)S(1)}, bf16[512,512]{1,0:T(8,128)(2,1)S(1)}) custom-call(f32[128,64]{1,0:T(8,128)S(1)} %get-tuple-element.41.sketch_ref.leaf_ref, f32[128,8192]{1,0:T(8,128)} %archive_ref.7, f32[128,512]{1,0:T(8,128)S(1)} %collective-permute-done.3.p1, f32[128,512]{1,0:T(8,128)S(1)} %collective-permute-done.4.p2, ...), custom_call_target="tpu_custom_call" | custom-call | flops 1073741824 | bytes 3145728 | tf_op jit(solution)/shard_map/grams/pallas_call | solution.py:223
  32.7 1.1 constant_dynamic-slice_fusion.3
  33.8 1.4 %collective-permute-start.6 = (f32[128,256]{1,0:T(8,128)S(1)}, f32[128,256]{1,0:T(8,128)S(1)}, u32[]{:S(2)}, u32[]{:S(2)}) collective-permute-start(f32[128,256]{1,0:T(8,128)S(1)} %get-tuple-element.72), channel_id=1, source_target_pairs={{0,1},{1,2},{2,3},{3,0},{4,5},{5,6},{6,7},{7,4},{8,9},{9,10},{10,1... | collective-permute-start | bytes 393224 | tf_op jit(solution)/shard_map/ppermute | solution.py:353
  35.2 3.7 %collective-permute-start.7 = (f32[128,256]{1,0:T(8,128)S(1)}, f32[128,256]{1,0:T(8,128)S(1)}, u32[]{:S(2)}, u32[]{:S(2)}) collective-permute-start(f32[128,256]{1,0:T(8,128)S(1)} %get-tuple-element.71), channel_id=1, source_target_pairs={{0,2},{1,3},{2,0},{3,1},{4,6},{5,7},{6,4},{7,5},{8,10},{9,11},{10,... | collective-permute-start | bytes 393224 | tf_op jit(solution)/shard_map/ppermute | solution.py:353
  39.0 6.9 %collective-permute-done.11.p3 = f32[128,768]{1,0:T(8,128)S(1)} collective-permute-done((f32[128,768]{1,0:T(8,128)}, f32[128,768]{1,0:T(8,128)S(1)}, u32[]{:S(2)}, u32[]{:S(2)}) %collective-permute-start.11) | collective-permute-done | bytes 393248 | tf_op jit(solution)/shard_map/ppermute | solution.py:353
  46.6 4.6 %grams.6 = (f32[512,128]{1,0:T(8,128)S(1)}, bf16[512,768]{1,0:T(8,128)(2,1)S(1)}, bf16[512,768]{1,0:T(8,128)(2,1)S(1)}) custom-call(f32[128,64]{1,0:T(8,128)S(1)} %get-tuple-element.41.sketch_ref.leaf_ref, f32[128,8192]{1,0:T(8,128)} %archive_ref.7, f32[128,768]{1,0:T(8,128)} %collective-permute-done.9.p1, f32[128,768]{1,0:T(8,128)S(1)} %collective-permute-done.10.p2, ...), custom_call_target="tpu_custom_call" | custom-call | flops 1610612736 | bytes 4718592 | tf_op jit(solution)/shard_map/grams/pallas_call | solution.py:223
  51.3 3.1 %grams.7 = (f32[256,128]{1,0:T(8,128)S(1)}, f32[256,128]{1,0:T(8,128)S(1)}, bf16[512,256]{1,0:T(8,128)(2,1)S(1)}, bf16[512,256]{1,0:T(8,128)(2,1)S(1)}) custom-call(f32[128,64]{1,0:T(8,128)S(1)} %get-tuple-element.41.sketch_ref.leaf_ref, f32[128,8192]{1,0:T(8,128)} %archive_ref.7, f32[128,256]{1,0:T(8,128)S(1)} %collective-permute-done.6.p1, ...), custom_call_target="tpu_custom_call" | custom-call | flops 536870912 | bytes 1572864 | tf_op jit(solution)/shard_map/grams/pallas_call | solution.py:223
  54.4 2.4 %collective-permute-start.12 = (f32[256,128]{1,0:T(8,128)S(1)}, f32[256,128]{1,0:T(8,128)S(1)}, u32[]{:S(2)}, u32[]{:S(2)}) collective-permute-start(f32[256,128]{1,0:T(8,128)S(1)} %get-tuple-element.54), channel_id=1, source_target_pairs={{0,4},{4,0},{1,5},{5,1},{2,6},{6,2},{3,7},{7,3},{8,12},{12,8},{9,1... | collective-permute-start | bytes 393224 | tf_op jit(solution)/shard_map/ppermute | solution.py:334
  56.8 1.0 collective-permute-done.12
  57.8 12.2 %all_to_all.15 = f32[16,16,128]{2,1,0:T(8,128)S(1)} all-to-all(f32[16,16,128]{2,1,0:T(8,128)S(1)} %bitcast.7), channel_id=1, replica_groups=mesh['z'=8,'x'=4,'core'=2,'tm'=4] {'x','tm'}, dimensions={0} | all-to-all | bytes 262144 | tf_op jit(solution)/shard_map/all_to_all | solution.py:322
  70.0 15.2 %all_to_all.16 = f32[8,16,128]{2,1,0:T(8,128)S(1)} all-to-all(f32[8,16,128]{2,1,0:T(8,128)S(1)} %broadcast_in_dim.4), channel_id=1, replica_groups=mesh['z'=8,'x'=4,'core'=2,'tm'=4] {'z'}, dimensions={0} | all-to-all | bytes 131072 | tf_op jit(solution)/shard_map/all_to_all | solution.py:322
  85.2 3.3 %collective-permute-start.13 = (f32[16,128]{1,0:T(8,128)S(1)}, f32[16,128]{1,0:T(8,128)S(1)}, u32[]{:S(2)}, u32[]{:S(2)}) collective-permute-start(f32[16,128]{1,0:T(8,128)S(1)} %reduce_sum.19), channel_id=1, source_target_pairs={{0,4},{4,0},{1,5},{5,1},{2,6},{6,2},{3,7},{7,3},{8,12},{12,8},{9,1... | collective-permute-start | bytes 24584 | tf_op jit(solution)/shard_map/ppermute | solution.py:337
  88.5 0.8 collective-permute-done.13
  89.4 10.7 %all_to_all.17 = f32[16,32,128]{2,1,0:T(8,128)S(1)} all-to-all(f32[16,32,128]{2,1,0:T(8,128)S(1)} %broadcast_in_dim.5), channel_id=1, replica_groups=mesh['z'=8,'x'=4,'core'=2,'tm'=4] {'x','tm'}, dimensions={0} | all-to-all | bytes 524288 | tf_op jit(solution)/shard_map/all_to_all | solution.py:322
  100.1 16.9 %modes.1 = (f32[16,2048]{1,0:T(8,128)S(1)}, f32[16,2048]{1,0:T(8,128)S(1)}, f32[16,2048]{1,0:T(8,128)S(1)}, f32[16,2048]{1,0:T(8,128)S(1)}) custom-call(f32[512,128]{1,0:T(8,128)S(1)} %bitcast.4, f32[128,64]{1,0:T(8,128)S(1)} %get-tuple-element.41.sketch_ref.leaf_ref, f32[64,128]{1,0:T(8,128)S(1)} %bitcast.6, bf16[512,512]{1,0:T(8,128)(2,1)} %get-tuple-element.55.refs_0_, ...), custom_call_target="tpu_custom_call" | custom-call | tf_op jit(solution)/shard_map/modes/pallas_call | solution.py:274
  117.4 1.6 %collective-permute-start.15 = (f32[16,2048]{1,0:T(8,128)S(1)}, f32[16,2048]{1,0:T(8,128)S(1)}, u32[]{:S(2)}, u32[]{:S(2)}) collective-permute-start(f32[16,2048]{1,0:T(8,128)S(1)} %get-tuple-element.65), channel_id=1, source_target_pairs={{0,2},{1,3},{2,0},{3,1},{4,6},{5,7},{6,4},{7,5},{8,10},{9,11},{10,... | collective-permute-start | bytes 393224 | tf_op jit(solution)/shard_map/ppermute | solution.py:375
  119.0 1.5 %collective-permute-start.16 = (f32[16,2048]{1,0:T(8,128)S(1)}, f32[16,2048]{1,0:T(8,128)S(1)}, u32[]{:S(2)}, u32[]{:S(2)}) collective-permute-start(f32[16,2048]{1,0:T(8,128)S(1)} %get-tuple-element.66), channel_id=1, source_target_pairs={{0,3},{1,0},{2,1},{3,2},{4,7},{5,4},{6,5},{7,6},{8,11},{9,8},{10,9... | collective-permute-start | bytes 393224 | tf_op jit(solution)/shard_map/ppermute | solution.py:375
  120.5 3.5 %collective-permute-done.14.p1 = f32[16,2048]{1,0:T(8,128)S(1)} collective-permute-done((f32[16,2048]{1,0:T(8,128)S(1)}, f32[16,2048]{1,0:T(8,128)S(1)}, u32[]{:S(2)}, u32[]{:S(2)}) %collective-permute-start.14) | collective-permute-done | bytes 131104 | tf_op jit(solution)/shard_map/ppermute | solution.py:375
  124.5 0.8 place.1
  (25 shorter events, 2.9 us)
Async XLA Ops:
  0.0 25.2 %copy-start = (f32[128,64]{0,1:T(8,128)S(1)}, f32[128,64]{0,1:T(8,128)}, u32[]{:S(2)}) copy-start(f32[128,64]{0,1:T(8,128)} %param.4) | copy-start | bytes 98308
  1.2 9.0 %collective-permute-start = (f32[128,512]{1,0:T(8,128)S(1)}, f32[128,512]{1,0:T(8,128)S(1)}, u32[]{:S(2)}, u32[]{:S(2)}) collective-permute-start(f32[128,512]{1,0:T(8,128)S(1)} %get-tuple-element.78), channel_id=1, source_target_pairs={{0,1},{1,2},{2,3},{3,0},{4,5},{5,6},{6,7},{7,4},{8,9},{9,10},{10,1... | collective-permute-start | bytes 786440 | tf_op jit(solution)/shard_map/ppermute | solution.py:353
  3.4 14.0 %collective-permute-start.1 = (f32[128,512]{1,0:T(8,128)S(1)}, f32[128,512]{1,0:T(8,128)S(1)}, u32[]{:S(2)}, u32[]{:S(2)}) collective-permute-start(f32[128,512]{1,0:T(8,128)S(1)} %get-tuple-element.77), channel_id=1, source_target_pairs={{0,2},{1,3},{2,0},{3,1},{4,6},{5,7},{6,4},{7,5},{8,10},{9,11},{10,... | collective-permute-start | bytes 786440 | tf_op jit(solution)/shard_map/ppermute | solution.py:353
  6.0 12.4 %collective-permute-start.2 = (f32[128,512]{1,0:T(8,128)S(1)}, f32[128,512]{1,0:T(8,128)S(1)}, u32[]{:S(2)}, u32[]{:S(2)}) collective-permute-start(f32[128,512]{1,0:T(8,128)S(1)} %get-tuple-element.76), channel_id=1, source_target_pairs={{0,3},{1,0},{2,1},{3,2},{4,7},{5,4},{6,5},{7,6},{8,11},{9,8},{10,9... | collective-permute-start | bytes 786440 | tf_op jit(solution)/shard_map/ppermute | solution.py:353
  8.9 15.7 %collective-permute-start.3 = (f32[128,512]{1,0:T(8,128)}, f32[128,512]{1,0:T(8,128)S(1)}, u32[]{:S(2)}, u32[]{:S(2)}) collective-permute-start(f32[128,512]{1,0:T(8,128)} %get-tuple-element.75), channel_id=1, source_target_pairs={{0,1},{1,2},{2,3},{3,0},{4,5},{5,6},{6,7},{7,4},{8,9},{9,10},{10,1... | collective-permute-start | bytes 786440 | tf_op jit(solution)/shard_map/ppermute | solution.py:353
  9.3 19.6 %collective-permute-start.4 = (f32[128,512]{1,0:T(8,128)S(1)}, f32[128,512]{1,0:T(8,128)S(1)}, u32[]{:S(2)}, u32[]{:S(2)}) collective-permute-start(f32[128,512]{1,0:T(8,128)S(1)} %get-tuple-element.74), channel_id=1, source_target_pairs={{0,2},{1,3},{2,0},{3,1},{4,6},{5,7},{6,4},{7,5},{8,10},{9,11},{10,... | collective-permute-start | bytes 786440 | tf_op jit(solution)/shard_map/ppermute | solution.py:353
  10.1 18.9 %collective-permute-start.5 = (f32[128,512]{1,0:T(8,128)S(1)}, f32[128,512]{1,0:T(8,128)S(1)}, u32[]{:S(2)}, u32[]{:S(2)}) collective-permute-start(f32[128,512]{1,0:T(8,128)S(1)} %get-tuple-element.73), channel_id=1, source_target_pairs={{0,3},{1,0},{2,1},{3,2},{4,7},{5,4},{6,5},{7,6},{8,11},{9,8},{10,9... | collective-permute-start | bytes 786440 | tf_op jit(solution)/shard_map/ppermute | solution.py:353
  20.7 18.3 %collective-permute-start.10 = (f32[128,768]{1,0:T(8,128)}, f32[128,768]{1,0:T(8,128)S(1)}, u32[]{:S(2)}, u32[]{:S(2)}) collective-permute-start(f32[128,768]{1,0:T(8,128)} %get-tuple-element.68), channel_id=1, source_target_pairs={{0,2},{1,3},{2,0},{3,1},{4,6},{5,7},{6,4},{7,5},{8,10},{9,11},{10,... | collective-permute-start | bytes 1179656 | tf_op jit(solution)/shard_map/ppermute | solution.py:353
  21.7 24.2 %collective-permute-start.11 = (f32[128,768]{1,0:T(8,128)}, f32[128,768]{1,0:T(8,128)S(1)}, u32[]{:S(2)}, u32[]{:S(2)}) collective-permute-start(f32[128,768]{1,0:T(8,128)} %get-tuple-element.67), channel_id=1, source_target_pairs={{0,3},{1,0},{2,1},{3,2},{4,7},{5,4},{6,5},{7,6},{8,11},{9,8},{10,9... | collective-permute-start | bytes 1179656 | tf_op jit(solution)/shard_map/ppermute | solution.py:353
  24.6 22.0 %collective-permute-start.9 = (f32[128,768]{1,0:T(8,128)}, f32[128,768]{1,0:T(8,128)}, u32[]{:S(2)}, u32[]{:S(2)}) collective-permute-start(f32[128,768]{1,0:T(8,128)} %get-tuple-element.69), channel_id=1, source_target_pairs={{0,1},{1,2},{2,3},{3,0},{4,5},{5,6},{6,7},{7,4},{8,9},{9,10},{10,1... | collective-permute-start | bytes 1179656 | tf_op jit(solution)/shard_map/ppermute | solution.py:353
  33.8 17.4 %collective-permute-start.6 = (f32[128,256]{1,0:T(8,128)S(1)}, f32[128,256]{1,0:T(8,128)S(1)}, u32[]{:S(2)}, u32[]{:S(2)}) collective-permute-start(f32[128,256]{1,0:T(8,128)S(1)} %get-tuple-element.72), channel_id=1, source_target_pairs={{0,1},{1,2},{2,3},{3,0},{4,5},{5,6},{6,7},{7,4},{8,9},{9,10},{10,1... | collective-permute-start | bytes 393224 | tf_op jit(solution)/shard_map/ppermute | solution.py:353
  35.2 16.0 %collective-permute-start.7 = (f32[128,256]{1,0:T(8,128)S(1)}, f32[128,256]{1,0:T(8,128)S(1)}, u32[]{:S(2)}, u32[]{:S(2)}) collective-permute-start(f32[128,256]{1,0:T(8,128)S(1)} %get-tuple-element.71), channel_id=1, source_target_pairs={{0,2},{1,3},{2,0},{3,1},{4,6},{5,7},{6,4},{7,5},{8,10},{9,11},{10,... | collective-permute-start | bytes 393224 | tf_op jit(solution)/shard_map/ppermute | solution.py:353
  39.0 12.3 %collective-permute-start.8 = (f32[128,256]{1,0:T(8,128)S(1)}, f32[128,256]{1,0:T(8,128)S(1)}, u32[]{:S(2)}, u32[]{:S(2)}) collective-permute-start(f32[128,256]{1,0:T(8,128)S(1)} %get-tuple-element.70), channel_id=1, source_target_pairs={{0,3},{1,0},{2,1},{3,2},{4,7},{5,4},{6,5},{7,6},{8,11},{9,8},{10,9... | collective-permute-start | bytes 393224 | tf_op jit(solution)/shard_map/ppermute | solution.py:353
  51.2 48.8 %copy-start.1 = (f32[128,64]{0,1:T(8,128)S(1)}, f32[128,64]{0,1:T(8,128)}, u32[]{:S(2)}) copy-start(f32[128,64]{0,1:T(8,128)} %param.5) | copy-start | bytes 98308
  54.4 3.4 %collective-permute-start.12 = (f32[256,128]{1,0:T(8,128)S(1)}, f32[256,128]{1,0:T(8,128)S(1)}, u32[]{:S(2)}, u32[]{:S(2)}) collective-permute-start(f32[256,128]{1,0:T(8,128)S(1)} %get-tuple-element.54), channel_id=1, source_target_pairs={{0,4},{4,0},{1,5},{5,1},{2,6},{6,2},{3,7},{7,3},{8,12},{12,8},{9,1... | collective-permute-start | bytes 393224 | tf_op jit(solution)/shard_map/ppermute | solution.py:334
  85.2 4.1 %collective-permute-start.13 = (f32[16,128]{1,0:T(8,128)S(1)}, f32[16,128]{1,0:T(8,128)S(1)}, u32[]{:S(2)}, u32[]{:S(2)}) collective-permute-start(f32[16,128]{1,0:T(8,128)S(1)} %reduce_sum.19), channel_id=1, source_target_pairs={{0,4},{4,0},{1,5},{5,1},{2,6},{6,2},{3,7},{7,3},{8,12},{12,8},{9,1... | collective-permute-start | bytes 24584 | tf_op jit(solution)/shard_map/ppermute | solution.py:337
  117.0 7.1 %collective-permute-start.14 = (f32[16,2048]{1,0:T(8,128)S(1)}, f32[16,2048]{1,0:T(8,128)S(1)}, u32[]{:S(2)}, u32[]{:S(2)}) collective-permute-start(f32[16,2048]{1,0:T(8,128)S(1)} %get-tuple-element.64), channel_id=1, source_target_pairs={{0,1},{1,2},{2,3},{3,0},{4,5},{5,6},{6,7},{7,4},{8,9},{9,10},{10,1... | collective-permute-start | bytes 393224 | tf_op jit(solution)/shard_map/ppermute | solution.py:375
  117.4 6.6 %collective-permute-start.15 = (f32[16,2048]{1,0:T(8,128)S(1)}, f32[16,2048]{1,0:T(8,128)S(1)}, u32[]{:S(2)}, u32[]{:S(2)}) collective-permute-start(f32[16,2048]{1,0:T(8,128)S(1)} %get-tuple-element.65), channel_id=1, source_target_pairs={{0,2},{1,3},{2,0},{3,1},{4,6},{5,7},{6,4},{7,5},{8,10},{9,11},{10,... | collective-permute-start | bytes 393224 | tf_op jit(solution)/shard_map/ppermute | solution.py:375
  119.0 5.5 %collective-permute-start.16 = (f32[16,2048]{1,0:T(8,128)S(1)}, f32[16,2048]{1,0:T(8,128)S(1)}, u32[]{:S(2)}, u32[]{:S(2)}) collective-permute-start(f32[16,2048]{1,0:T(8,128)S(1)} %get-tuple-element.66), channel_id=1, source_target_pairs={{0,3},{1,0},{2,1},{3,2},{4,7},{5,4},{6,5},{7,6},{8,11},{9,8},{10,9... | collective-permute-start | bytes 393224 | tf_op jit(solution)/shard_map/ppermute | solution.py:375
